TPU v7x, 32 devices: a whole 2x2x4 slice. The times are simulated.
32 devices in a mesh: probe: 2 (over y), lon: 4 (over z), lat: 2 (over core), trc: 2 (over x).
Axes of the slice: x: 2, y: 2, z: 4, core: 2. Of those that a mesh axis runs over, the one named last changes fastest.
Arguments:
- probe_signs: int32 [24, 2, 32, 256], P(('probe', 'trc'), None, 'lon', 'lat'), parts along dimension 0, may hold values from 0 to 1
- shift_cells: int32 [2, 256], P(None, 'lat'), may hold values from 1 to 31, as said below
- courant_frac: float32 [2, 256], P(None, 'lat'), may hold values from 0 to 1
- merid_coef: float32 [2, 256], P(None, 'lat'), may hold values from 0 to 0.24
- convect_frac: float32 [32, 256], P('lon', 'lat'), may hold values from 0 to 0.9
- footprint: float32 [32, 256], P('lon', 'lat'), may hold values from 0.3 to 3
- region_id: int32 [32, 256], P('lon', 'lat'), may hold values from 0 to 31
- owner_slots: int32 [32], replicated, may hold values from 0 to 31, each once
- prior_slot: float32 [12, 32], P('trc'), may hold values from 0.0125 to 0.1875
Outputs:
- diag_estimate: float32 [24, 2, 32, 256], P(('probe', 'trc'), None, 'lon', 'lat'), parts along dimension 0
There are 2 independent parts, one for each index of `probe`. A program takes and returns all parts, laid end to end along the dimension named above; an argument that names none is the same for every part. Nothing has to cross between parts.
Inputs may be any that keep to these rules, and one draw needn't show every extreme that they name: `shift_cells`: rows below 32 and from 224 on hold shifts of 8 or more at every level; all other rows hold shifts below 8.
All inputs are finite; a program needn't handle non-finite values.
Results may differ from a plain program's by a relative error of at most 0.00011.
Values sent between devices are 32-bit elements; how exact they have to be, the bound alone decides.
No kernel may reach another device: no remote copies, remote signals or barrier semaphores. Data moves between devices by JAX's collectives and lax.ppermute only.
A program may use at most 64 MiB of HBM per device.

v0:
```python
import jax
import jax.numpy as jnp
from jax import lax
from jax.sharding import PartitionSpec as P


def from_behind(block, axis, distance):
    devices = range(lax.axis_size(axis))
    route = [((i - distance) % len(devices), i) for i in devices]
    return lax.ppermute(block, axis, route)


def extended(value, sides, width, wrap):
    for axis, dim in sides:
        size, length = (lax.axis_size(axis), value.shape[dim])
        up = [(i, (i + 1) % size) for i in range(size if wrap else size - 1)]
        down = [(j, i) for i, j in up]
        last = lax.slice_in_dim(value, length - width, length, axis=dim)
        first = lax.slice_in_dim(value, 0, width, axis=dim)
        before = lax.ppermute(last, axis, up)
        after = lax.ppermute(first, axis, down)
        value = jnp.concatenate([before, value, after], axis=dim)
    return value


def from_behind_2(value, axis, by):
    size = lax.axis_size(axis)
    pairs = [(i, i + by) for i in range(size) if 0 <= i + by < size]
    return lax.ppermute(value, axis, pairs)


def rotate_every(field, blocks, direction):
    cycle_size = lax.axis_size("lon")
    for bit_number in range((cycle_size - 1).bit_length()):
        moved = from_behind(field, "lon", direction * (1 << bit_number))
        chosen = (blocks >> bit_number & 1)[None, :, None, :] == 1
        field = jnp.where(chosen, moved, field)
    return field


def cycle_move(field, blocks, direction):
    return rotate_every(field, blocks, direction)


def neighbour_join(field, direction):
    other = from_behind(field, "lon", direction)
    if direction == 1:
        return jnp.concatenate([other, field], axis=2)
    return jnp.concatenate([field, other], axis=2)


def slide_cells(joined, within, width, forward):
    current = joined
    for bit_number in range(max(width - 1, 1).bit_length()):
        step = 1 << bit_number
        pad = jnp.zeros(current.shape[:2] + (step,) + current.shape[3:], current.dtype)
        if forward:
            moved = jnp.concatenate([pad, current[:, :, :-step]], axis=2)
        else:
            moved = jnp.concatenate([current[:, :, step:], pad], axis=2)
        chosen = (within >> bit_number & 1)[None, :, None, :] == 1
        current = jnp.where(chosen, moved, current)
    if forward:
        return current[:, :, width:]
    return current[:, :, :width]


def lon_padded(field):
    return extended(field, (("lon", 2),), 1, True)


def zonal_weights(courant_frac):
    frac = courant_frac[None, :, None, :]
    return (frac * (frac + 1.0) / 2.0, 1.0 - frac * frac, -frac * (1.0 - frac) / 2.0)


def zonal_forward(field, courant_frac, blocks, within):
    w_left, w_centre, w_right = zonal_weights(courant_frac)
    padded = lon_padded(field)
    stencil = w_left * padded[:, :, :-2] + w_centre * field + w_right * padded[:, :, 2:]
    joined = neighbour_join(cycle_move(stencil, blocks, 1), 1)
    return slide_cells(joined, within, field.shape[2], True)


def zonal_adjoint(field, courant_frac, blocks, within):
    w_left, w_centre, w_right = zonal_weights(courant_frac)
    joined = neighbour_join(cycle_move(field, blocks, -1), -1)
    moved = slide_cells(joined, within, field.shape[2], False)
    padded = lon_padded(moved)
    return w_left * padded[:, :, 2:] + w_centre * moved + w_right * padded[:, :, :-2]


def meridional(field, faces, faces_prev):
    padded = extended(field, (("lat", 3),), 1, False)
    flux_here = faces[None, :, None, :] * (padded[..., 2:] - field)
    flux_prev = faces_prev[None, :, None, :] * (field - padded[..., :-2])
    return field + flux_here - flux_prev


def convective(field, convect_frac):
    column = jnp.mean(field, axis=1, keepdims=True)
    return field + convect_frac[None, None] * (column - field)


def on_device(
    probe_signs,
    shift_cells,
    courant_frac,
    merid_coef,
    convect_frac,
    footprint,
    region_id,
    owner_slots,
    prior_slot,
):
    tracers, levels, width, rows = probe_signs.shape
    band = lax.axis_index("lat")
    global_rows = band * rows + jnp.arange(rows, dtype=jnp.int32)
    last_row = lax.axis_size("lat") * rows - 1
    faces = jnp.where((global_rows == last_row)[None, :], 0.0, merid_coef)
    below = from_behind_2(faces[:, -1:], "lat", 1)
    faces_prev = jnp.concatenate([below, faces[:, :-1]], axis=1)
    blocks = shift_cells // width
    within = shift_cells % width
    probe = (2 * probe_signs - 1).astype(jnp.float32)
    adjoint = probe
    for turn in range(2):
        mixed = meridional(convective(adjoint, convect_frac), faces, faces_prev)
        adjoint = zonal_adjoint(mixed, courant_frac, blocks, within)
    bottom = footprint[None] * adjoint[:, 0]
    regions = owner_slots.shape[0]
    region_table = (
        region_id.reshape(-1)[:, None] == jnp.arange(regions, dtype=jnp.int32)[None, :]
    ).astype(jnp.float32)
    partial_value = jnp.dot(
        bottom.reshape(tracers, width * rows),
        region_table,
        precision=lax.Precision.HIGHEST,
        preferred_element_type=jnp.float32,
    )
    slot_sums = partial_value[:, owner_slots]
    scaled = lax.psum(slot_sums, ("lon", "lat")) * prior_slot
    by_region = jnp.zeros((tracers, regions), jnp.float32).at[:, owner_slots].set(scaled)
    spread = lax.dot_general(
        by_region,
        region_table,
        (((1,), (1,)), ((), ())),
        precision=lax.Precision.HIGHEST,
        preferred_element_type=jnp.float32,
    )
    surface = footprint[None] * spread.reshape(tracers, width, rows)
    source = jnp.concatenate(
        [surface[:, None], jnp.zeros((tracers, levels - 1, width, rows), jnp.float32)], axis=1
    )
    for turn in range(2):
        moved = zonal_forward(source, courant_frac, blocks, within)
        source = convective(meridional(moved, faces, faces_prev), convect_frac)
    return probe * source


def solution(mesh):
    placed = (
        P(("probe", "trc"), None, "lon", "lat"),
        P(None, "lat"),
        P(None, "lat"),
        P(None, "lat"),
        P("lon", "lat"),
        P("lon", "lat"),
        P("lon", "lat"),
        P(),
        P("trc", None),
    )
    return jax.shard_map(
        on_device,
        mesh=mesh,
        in_specs=placed,
        out_specs=P(("probe", "trc"), None, "lon", "lat"),
        check_vma=False,
    )
```

profile of v0, /device:TPU:0, one launch (start us, length us, event | category | flops | bytes accessed | tf_op | source)
XLA Modules:
  0.0 151.1 jit_solution(5057359106431355183)
XLA Ops:
  0.0 0.7 copy-done.4
  0.7 0.1 slice.179
  0.8 2.5 %collective-permute-start.1 = (f32[2,1]{1,0:T(2,128)S(1)}, f32[2,1]{1,0:T(2,128)S(1)}, u32[]{:S(2)}, u32[]{:S(2)}) collective-permute-start(f32[2,1]{1,0:T(2,128)S(1)} %slice.179), channel_id=1, source_target_pairs={{0,2},{1,3},{4,6},{5,7},{8,10},{9,11},{12,14},{13,15},{16,18},{17,... | collective-permute-start | bytes 32 | tf_op jit(solution)/shard_map/ppermute | solution.py:29
  3.2 0.8 convert_reduce_fusion
  4.1 0.7 copy-done.1
  4.8 0.1 fusion.71
  4.8 1.4 collective-permute-start
  6.3 3.0 %collective-permute-start.2 = (f32[6,2,8,1]{3,2,1,0:T(8,128)S(1)}, f32[6,2,8,1]{3,2,1,0:T(8,128)S(1)}, u32[]{:S(2)}, u32[]{:S(2)}) collective-permute-start(f32[6,2,8,1]{3,2,1,0:T(8,128)S(1)} %get-tuple-element.26), channel_id=1, source_target_pairs={{0,2},{1,3},{4,6},{5,7},{8,10},{9,11},{12,14},{13,15},{16,18},{17,... | collective-permute-start | bytes 1160 | tf_op jit(solution)/shard_map/ppermute | solution.py:20
  9.4 0.1 pad_maximum_fusion.20
  9.4 0.7 collective-permute-done.2
  10.2 0.1 fusion.43
  10.3 4.5 %collective-permute-start.3 = (f32[6,2,8,128]{3,2,1,0:T(8,128)S(1)}, f32[6,2,8,128]{3,2,1,0:T(8,128)S(1)}, u32[]{:S(2)}, u32[]{:S(2)}) collective-permute-start(f32[6,2,8,128]{3,2,1,0:T(8,128)S(1)} %fusion.43), channel_id=1, source_target_pairs={{4,0},{8,4},{12,8},{0,12},{5,1},{9,5},{13,9},{1,13},{6,2},{10,6},{... | collective-permute-start | bytes 147464 | tf_op jit(solution)/shard_map/ppermute | solution.py:10
  14.8 1.7 %collective-permute-done.3 = f32[6,2,8,128]{3,2,1,0:T(8,128)S(1)} collective-permute-done((f32[6,2,8,128]{3,2,1,0:T(8,128)S(1)}, f32[6,2,8,128]{3,2,1,0:T(8,128)S(1)}, u32[]{:S(2)}, u32[]{:S(2)}) %collective-permute-start.3) | collective-permute-done | bytes 49184 | tf_op jit(solution)/shard_map/ppermute | solution.py:10
  16.5 0.1 broadcast_select_fusion.3
  16.6 1.4 collective-permute-start.4
  18.0 3.9 %collective-permute-done.4 = f32[6,2,8,128]{3,2,1,0:T(8,128)S(1)} collective-permute-done((f32[6,2,8,128]{3,2,1,0:T(8,128)S(1)}, f32[6,2,8,128]{3,2,1,0:T(8,128)S(1)}, u32[]{:S(2)}, u32[]{:S(2)}) %collective-permute-start.4) | collective-permute-done | bytes 49184 | tf_op jit(solution)/shard_map/ppermute | solution.py:10
  22.0 3.9 %collective-permute-start.5 = (f32[6,2,8,128]{3,2,1,0:T(8,128)S(1)}, f32[6,2,8,128]{3,2,1,0:T(8,128)S(1)}, u32[]{:S(2)}, u32[]{:S(2)}) collective-permute-start(f32[6,2,8,128]{3,2,1,0:T(8,128)S(1)} %broadcast_select_fusion.7), channel_id=1, source_target_pairs={{4,0},{8,4},{12,8},{0,12},{5,1},{9,5},{13,9},{1,13},{6,2},{10,6},{... | collective-permute-start | bytes 147464 | tf_op jit(solution)/shard_map/ppermute | solution.py:10
  25.9 1.7 %collective-permute-done.5 = f32[6,2,8,128]{3,2,1,0:T(8,128)S(1)} collective-permute-done((f32[6,2,8,128]{3,2,1,0:T(8,128)S(1)}, f32[6,2,8,128]{3,2,1,0:T(8,128)S(1)}, u32[]{:S(2)}, u32[]{:S(2)}) %collective-permute-start.5) | collective-permute-done | bytes 49184 | tf_op jit(solution)/shard_map/ppermute | solution.py:10
  27.8 4.2 %collective-permute-start.6 = (f32[6,2,1,128]{3,2,1,0:T(1,128)S(1)}, f32[6,2,1,128]{3,2,1,0:T(1,128)S(1)}, u32[]{:S(2)}, u32[]{:S(2)}) collective-permute-start(f32[6,2,1,128]{3,2,1,0:T(1,128)S(1)} %get-tuple-element.19), channel_id=1, source_target_pairs={{4,0},{8,4},{12,8},{0,12},{5,1},{9,5},{13,9},{1,13},{6,2},{10,6},{... | collective-permute-start | bytes 18440 | tf_op jit(solution)/shard_map/ppermute | solution.py:21
  32.0 1.3 collective-permute-done.6
  33.3 4.1 %collective-permute-done.7 = f32[6,2,1,128]{3,2,1,0:T(1,128)S(1)} collective-permute-done((f32[6,2,1,128]{3,2,1,0:T(1,128)S(1)}, f32[6,2,1,128]{3,2,1,0:T(1,128)S(1)}, u32[]{:S(2)}, u32[]{:S(2)}) %collective-permute-start.7) | collective-permute-done | bytes 6176 | tf_op jit(solution)/shard_map/ppermute | solution.py:20
  37.5 0.1 fusion.70
  37.6 1.3 collective-permute-start.8
  38.9 3.0 %collective-permute-start.9 = (f32[6,2,8,1]{3,2,1,0:T(8,128)S(1)}, f32[6,2,8,1]{3,2,1,0:T(8,128)S(1)}, u32[]{:S(2)}, u32[]{:S(2)}) collective-permute-start(f32[6,2,8,1]{3,2,1,0:T(8,128)S(1)} %get-tuple-element.24), channel_id=1, source_target_pairs={{0,2},{1,3},{4,6},{5,7},{8,10},{9,11},{12,14},{13,15},{16,18},{17,... | collective-permute-start | bytes 1160 | tf_op jit(solution)/shard_map/ppermute | solution.py:20
  41.9 0.9 collective-permute-done.9
  42.8 0.1 fusion.33
  43.0 4.1 %collective-permute-done.10 = f32[6,2,8,128]{3,2,1,0:T(8,128)S(1)} collective-permute-done((f32[6,2,8,128]{3,2,1,0:T(8,128)S(1)}, f32[6,2,8,128]{3,2,1,0:T(8,128)S(1)}, u32[]{:S(2)}, u32[]{:S(2)}) %collective-permute-start.10) | collective-permute-done | bytes 49184 | tf_op jit(solution)/shard_map/ppermute | solution.py:10
  47.0 0.1 broadcast_select_fusion.2
  47.3 5.0 %collective-permute-done.11 = f32[6,2,8,128]{3,2,1,0:T(8,128)S(1)} collective-permute-done((f32[6,2,8,128]{3,2,1,0:T(8,128)S(1)}, f32[6,2,8,128]{3,2,1,0:T(8,128)S(1)}, u32[]{:S(2)}, u32[]{:S(2)}) %collective-permute-start.11) | collective-permute-done | bytes 49184 | tf_op jit(solution)/shard_map/ppermute | solution.py:10
  52.2 2.0 %collective-permute-start.12 = (f32[6,2,8,128]{3,2,1,0:T(8,128)S(1)}, f32[6,2,8,128]{3,2,1,0:T(8,128)S(1)}, u32[]{:S(2)}, u32[]{:S(2)}) collective-permute-start(f32[6,2,8,128]{3,2,1,0:T(8,128)S(1)} %broadcast_select_fusion.6), channel_id=1, source_target_pairs={{4,0},{8,4},{12,8},{0,12},{5,1},{9,5},{13,9},{1,13},{6,2},{10,6},{... | collective-permute-start | bytes 147464 | tf_op jit(solution)/shard_map/ppermute | solution.py:10
  54.3 2.1 %collective-permute-done.12 = f32[6,2,8,128]{3,2,1,0:T(8,128)S(1)} collective-permute-done((f32[6,2,8,128]{3,2,1,0:T(8,128)S(1)}, f32[6,2,8,128]{3,2,1,0:T(8,128)S(1)}, u32[]{:S(2)}, u32[]{:S(2)}) %collective-permute-start.12) | collective-permute-done | bytes 49184 | tf_op jit(solution)/shard_map/ppermute | solution.py:10
  56.5 3.8 %collective-permute-start.13 = (f32[6,2,1,128]{3,2,1,0:T(1,128)S(1)}, f32[6,2,1,128]{3,2,1,0:T(1,128)S(1)}, u32[]{:S(2)}, u32[]{:S(2)}) collective-permute-start(f32[6,2,1,128]{3,2,1,0:T(1,128)S(1)} %get-tuple-element.17), channel_id=1, source_target_pairs={{4,0},{8,4},{12,8},{0,12},{5,1},{9,5},{13,9},{1,13},{6,2},{10,6},{... | collective-permute-start | bytes 18440 | tf_op jit(solution)/shard_map/ppermute | solution.py:21
  60.4 0.6 copy-done.2
  61.1 0.1 copy.10
  61.2 0.6 collective-permute-done.13
  61.7 4.1 %collective-permute-done.14 = f32[6,2,1,128]{3,2,1,0:T(1,128)S(1)} collective-permute-done((f32[6,2,1,128]{3,2,1,0:T(1,128)S(1)}, f32[6,2,1,128]{3,2,1,0:T(1,128)S(1)}, u32[]{:S(2)}, u32[]{:S(2)}) %collective-permute-start.14) | collective-permute-done | bytes 6176 | tf_op jit(solution)/shard_map/ppermute | solution.py:20
  65.8 0.7 fusion
  66.6 0.6 gather_fusion
  67.1 25.9 %psum.7 = f32[6,32]{0,1:T(8,128)S(1)} all-reduce(f32[6,32]{0,1:T(8,128)S(1)} %bitcast.35), channel_id=1, replica_groups=mesh['probe'=2,'lon'=4,'lat'=2,'trc'=2] {'lon','lat'}, use_global_device_ids=true, to_apply=%region_2.3 | all-reduce | flops 192 | bytes 1536 | tf_op jit(solution)/shard_map/psum | solution.py:142
  93.1 0.7 scatter_custom_fusion
  93.7 0.5 convolution_bitcast_fusion
  94.3 3.8 %collective-permute-start.16 = (f32[6,2,1,128]{3,2,1,0:T(1,128)S(1)}, f32[6,2,1,128]{3,2,1,0:T(1,128)S(1)}, u32[]{:S(2)}, u32[]{:S(2)}) collective-permute-start(f32[6,2,1,128]{3,2,1,0:T(1,128)S(1)} %get-tuple-element.28), channel_id=1, source_target_pairs={{4,0},{8,4},{12,8},{0,12},{5,1},{9,5},{13,9},{1,13},{6,2},{10,6},{... | collective-permute-start | bytes 18440 | tf_op jit(solution)/shard_map/ppermute | solution.py:21
  98.1 1.7 %collective-permute-done.15 = f32[6,2,1,128]{3,2,1,0:T(1,128)S(1)} collective-permute-done((f32[6,2,1,128]{3,2,1,0:T(1,128)S(1)}, f32[6,2,1,128]{3,2,1,0:T(1,128)S(1)}, u32[]{:S(2)}, u32[]{:S(2)}) %collective-permute-start.15) | collective-permute-done | bytes 6176 | tf_op jit(solution)/shard_map/ppermute | solution.py:20
  99.9 5.9 %collective-permute-done.17 = f32[6,2,8,128]{3,2,1,0:T(8,128)S(1)} collective-permute-done((f32[6,2,8,128]{3,2,1,0:T(8,128)S(1)}, f32[6,2,8,128]{3,2,1,0:T(8,128)S(1)}, u32[]{:S(2)}, u32[]{:S(2)}) %collective-permute-start.17) | collective-permute-done | bytes 49184 | tf_op jit(solution)/shard_map/ppermute | solution.py:10
  105.8 0.2 collective-permute-start.18
  106.1 4.8 %collective-permute-done.18 = f32[6,2,8,128]{3,2,1,0:T(8,128)S(1)} collective-permute-done((f32[6,2,8,128]{3,2,1,0:T(8,128)S(1)}, f32[6,2,8,128]{3,2,1,0:T(8,128)S(1)}, u32[]{:S(2)}, u32[]{:S(2)}) %collective-permute-start.18) | collective-permute-done | bytes 49184 | tf_op jit(solution)/shard_map/ppermute | solution.py:10
  111.0 5.9 %collective-permute-done.19 = f32[6,2,8,128]{3,2,1,0:T(8,128)S(1)} collective-permute-done((f32[6,2,8,128]{3,2,1,0:T(8,128)S(1)}, f32[6,2,8,128]{3,2,1,0:T(8,128)S(1)}, u32[]{:S(2)}, u32[]{:S(2)}) %collective-permute-start.19) | collective-permute-done | bytes 49184 | tf_op jit(solution)/shard_map/ppermute | solution.py:10
  116.9 0.1 fusion.66
  117.0 1.3 collective-permute-start.20
  118.3 3.0 %collective-permute-start.21 = (f32[6,2,8,1]{3,2,1,0:T(8,128)S(1)}, f32[6,2,8,1]{3,2,1,0:T(8,128)S(1)}, u32[]{:S(2)}, u32[]{:S(2)}) collective-permute-start(f32[6,2,8,1]{3,2,1,0:T(8,128)S(1)} %get-tuple-element.16), channel_id=1, source_target_pairs={{0,2},{1,3},{4,6},{5,7},{8,10},{9,11},{12,14},{13,15},{16,18},{17,... | collective-permute-start | bytes 1160 | tf_op jit(solution)/shard_map/ppermute | solution.py:20
  121.3 0.8 collective-permute-done.21
  122.2 0.1 fusion.63
  122.4 3.8 %collective-permute-start.23 = (f32[6,2,1,128]{3,2,1,0:T(1,128)S(1)}, f32[6,2,1,128]{3,2,1,0:T(1,128)S(1)}, u32[]{:S(2)}, u32[]{:S(2)}) collective-permute-start(f32[6,2,1,128]{3,2,1,0:T(1,128)S(1)} %get-tuple-element.22), channel_id=1, source_target_pairs={{4,0},{8,4},{12,8},{0,12},{5,1},{9,5},{13,9},{1,13},{6,2},{10,6},{... | collective-permute-start | bytes 18440 | tf_op jit(solution)/shard_map/ppermute | solution.py:21
  126.2 1.6 %collective-permute-done.22 = f32[6,2,1,128]{3,2,1,0:T(1,128)S(1)} collective-permute-done((f32[6,2,1,128]{3,2,1,0:T(1,128)S(1)}, f32[6,2,1,128]{3,2,1,0:T(1,128)S(1)}, u32[]{:S(2)}, u32[]{:S(2)}) %collective-permute-start.22) | collective-permute-done | bytes 6176 | tf_op jit(solution)/shard_map/ppermute | solution.py:20
  127.9 6.0 %collective-permute-done.24 = f32[6,2,8,128]{3,2,1,0:T(8,128)S(1)} collective-permute-done((f32[6,2,8,128]{3,2,1,0:T(8,128)S(1)}, f32[6,2,8,128]{3,2,1,0:T(8,128)S(1)}, u32[]{:S(2)}, u32[]{:S(2)}) %collective-permute-start.24) | collective-permute-done | bytes 49184 | tf_op jit(solution)/shard_map/ppermute | solution.py:10
  134.0 0.3 collective-permute-start.25
  134.3 4.7 %collective-permute-done.25 = f32[6,2,8,128]{3,2,1,0:T(8,128)S(1)} collective-permute-done((f32[6,2,8,128]{3,2,1,0:T(8,128)S(1)}, f32[6,2,8,128]{3,2,1,0:T(8,128)S(1)}, u32[]{:S(2)}, u32[]{:S(2)}) %collective-permute-start.25) | collective-permute-done | bytes 49184 | tf_op jit(solution)/shard_map/ppermute | solution.py:10
  139.1 5.9 %collective-permute-done.26 = f32[6,2,8,128]{3,2,1,0:T(8,128)S(1)} collective-permute-done((f32[6,2,8,128]{3,2,1,0:T(8,128)S(1)}, f32[6,2,8,128]{3,2,1,0:T(8,128)S(1)}, u32[]{:S(2)}, u32[]{:S(2)}) %collective-permute-start.26) | collective-permute-done | bytes 49184 | tf_op jit(solution)/shard_map/ppermute | solution.py:10
  145.0 0.1 fusion.65
  145.1 1.3 collective-permute-start.27
  146.4 3.0 %collective-permute-start.28 = (f32[6,2,8,1]{3,2,1,0:T(8,128)S(1)}, f32[6,2,8,1]{3,2,1,0:T(8,128)S(1)}, u32[]{:S(2)}, u32[]{:S(2)}) collective-permute-start(f32[6,2,8,1]{3,2,1,0:T(8,128)S(1)} %get-tuple-element.14), channel_id=1, source_target_pairs={{0,2},{1,3},{4,6},{5,7},{8,10},{9,11},{12,14},{13,15},{16,18},{17,... | collective-permute-start | bytes 1160 | tf_op jit(solution)/shard_map/ppermute | solution.py:20
  149.5 0.8 collective-permute-done.28
  150.3 0.1 fusion.61
  150.4 0.6 add_multiply_fusion
  (90 shorter events, 1.3 us)
Async XLA Ops:
  0.0 0.7 copy-start.4
  0.8 3.3 %copy-start = (s32[6,2,8,128]{3,2,1,0:T(8,128)S(1)}, s32[6,2,8,128]{3,2,1,0:T(8,128)}, u32[]{:S(2)}) copy-start(s32[6,2,8,128]{3,2,1,0:T(8,128)} %param.9) | copy-start | bytes 147460
  0.8 8.6 %collective-permute-start.1 = (f32[2,1]{1,0:T(2,128)S(1)}, f32[2,1]{1,0:T(2,128)S(1)}, u32[]{:S(2)}, u32[]{:S(2)}) collective-permute-start(f32[2,1]{1,0:T(2,128)S(1)} %slice.179), channel_id=1, source_target_pairs={{0,2},{1,3},{4,6},{5,7},{8,10},{9,11},{12,14},{13,15},{16,18},{17,... | collective-permute-start | bytes 32 | tf_op jit(solution)/shard_map/ppermute | solution.py:29
  4.1 0.7 copy-start.1
  4.8 4.5 %copy-start.5 = (s32[2,128]{1,0:T(2,128)S(1)}, s32[2,128]{1,0:T(2,128)}, u32[]{:S(2)}) copy-start(s32[2,128]{1,0:T(2,128)} %param.10) | copy-start | bytes 3076
  4.8 4.6 %collective-permute-start = (f32[6,2,8,1]{3,2,1,0:T(8,128)S(1)}, f32[6,2,8,1]{3,2,1,0:T(8,128)S(1)}, u32[]{:S(2)}, u32[]{:S(2)}) collective-permute-start(f32[6,2,8,1]{3,2,1,0:T(8,128)S(1)} %get-tuple-element.25), channel_id=1, source_target_pairs={{2,0},{3,1},{6,4},{7,5},{10,8},{11,9},{14,12},{15,13},{18,16},{19,... | collective-permute-start | bytes 1160 | tf_op jit(solution)/shard_map/ppermute | solution.py:21
  6.3 3.9 %collective-permute-start.2 = (f32[6,2,8,1]{3,2,1,0:T(8,128)S(1)}, f32[6,2,8,1]{3,2,1,0:T(8,128)S(1)}, u32[]{:S(2)}, u32[]{:S(2)}) collective-permute-start(f32[6,2,8,1]{3,2,1,0:T(8,128)S(1)} %get-tuple-element.26), channel_id=1, source_target_pairs={{0,2},{1,3},{4,6},{5,7},{8,10},{9,11},{12,14},{13,15},{16,18},{17,... | collective-permute-start | bytes 1160 | tf_op jit(solution)/shard_map/ppermute | solution.py:20
  10.3 6.2 %collective-permute-start.3 = (f32[6,2,8,128]{3,2,1,0:T(8,128)S(1)}, f32[6,2,8,128]{3,2,1,0:T(8,128)S(1)}, u32[]{:S(2)}, u32[]{:S(2)}) collective-permute-start(f32[6,2,8,128]{3,2,1,0:T(8,128)S(1)} %fusion.43), channel_id=1, source_target_pairs={{4,0},{8,4},{12,8},{0,12},{5,1},{9,5},{13,9},{1,13},{6,2},{10,6},{... | collective-permute-start | bytes 147464 | tf_op jit(solution)/shard_map/ppermute | solution.py:10
  16.6 5.3 %collective-permute-start.4 = (f32[6,2,8,128]{3,2,1,0:T(8,128)S(1)}, f32[6,2,8,128]{3,2,1,0:T(8,128)S(1)}, u32[]{:S(2)}, u32[]{:S(2)}) collective-permute-start(f32[6,2,8,128]{3,2,1,0:T(8,128)S(1)} %broadcast_select_fusion.3), channel_id=1, source_target_pairs={{8,0},{12,4},{0,8},{4,12},{9,1},{13,5},{1,9},{5,13},{10,2},{14,6},... | collective-permute-start | bytes 147464 | tf_op jit(solution)/shard_map/ppermute | solution.py:10
  22.0 5.7 %collective-permute-start.5 = (f32[6,2,8,128]{3,2,1,0:T(8,128)S(1)}, f32[6,2,8,128]{3,2,1,0:T(8,128)S(1)}, u32[]{:S(2)}, u32[]{:S(2)}) collective-permute-start(f32[6,2,8,128]{3,2,1,0:T(8,128)S(1)} %broadcast_select_fusion.7), channel_id=1, source_target_pairs={{4,0},{8,4},{12,8},{0,12},{5,1},{9,5},{13,9},{1,13},{6,2},{10,6},{... | collective-permute-start | bytes 147464 | tf_op jit(solution)/shard_map/ppermute | solution.py:10
  27.8 4.2 %copy-start.6 = (f32[2,128]{1,0:T(2,128)S(1)}, f32[2,128]{1,0:T(2,128)}, u32[]{:S(2)}) copy-start(f32[2,128]{1,0:T(2,128)} %param.11) | copy-start | bytes 3076
  27.8 5.5 %collective-permute-start.6 = (f32[6,2,1,128]{3,2,1,0:T(1,128)S(1)}, f32[6,2,1,128]{3,2,1,0:T(1,128)S(1)}, u32[]{:S(2)}, u32[]{:S(2)}) collective-permute-start(f32[6,2,1,128]{3,2,1,0:T(1,128)S(1)} %get-tuple-element.19), channel_id=1, source_target_pairs={{4,0},{8,4},{12,8},{0,12},{5,1},{9,5},{13,9},{1,13},{6,2},{10,6},{... | collective-permute-start | bytes 18440 | tf_op jit(solution)/shard_map/ppermute | solution.py:21
  32.0 5.4 %collective-permute-start.7 = (f32[6,2,1,128]{3,2,1,0:T(1,128)S(1)}, f32[6,2,1,128]{3,2,1,0:T(1,128)S(1)}, u32[]{:S(2)}, u32[]{:S(2)}) collective-permute-start(f32[6,2,1,128]{3,2,1,0:T(1,128)S(1)} %get-tuple-element.20), channel_id=1, source_target_pairs={{0,4},{4,8},{8,12},{12,0},{1,5},{5,9},{9,13},{13,1},{2,6},{6,10},{... | collective-permute-start | bytes 18440 | tf_op jit(solution)/shard_map/ppermute | solution.py:20
  37.6 4.3 %collective-permute-start.8 = (f32[6,2,8,1]{3,2,1,0:T(8,128)S(1)}, f32[6,2,8,1]{3,2,1,0:T(8,128)S(1)}, u32[]{:S(2)}, u32[]{:S(2)}) collective-permute-start(f32[6,2,8,1]{3,2,1,0:T(8,128)S(1)} %get-tuple-element.23), channel_id=1, source_target_pairs={{2,0},{3,1},{6,4},{7,5},{10,8},{11,9},{14,12},{15,13},{18,16},{19,... | collective-permute-start | bytes 1160 | tf_op jit(solution)/shard_map/ppermute | solution.py:21
  38.9 3.9 %collective-permute-start.9 = (f32[6,2,8,1]{3,2,1,0:T(8,128)S(1)}, f32[6,2,8,1]{3,2,1,0:T(8,128)S(1)}, u32[]{:S(2)}, u32[]{:S(2)}) collective-permute-start(f32[6,2,8,1]{3,2,1,0:T(8,128)S(1)} %get-tuple-element.24), channel_id=1, source_target_pairs={{0,2},{1,3},{4,6},{5,7},{8,10},{9,11},{12,14},{13,15},{16,18},{17,... | collective-permute-start | bytes 1160 | tf_op jit(solution)/shard_map/ppermute | solution.py:20
  42.9 4.1 %collective-permute-start.10 = (f32[6,2,8,128]{3,2,1,0:T(8,128)S(1)}, f32[6,2,8,128]{3,2,1,0:T(8,128)S(1)}, u32[]{:S(2)}, u32[]{:S(2)}) collective-permute-start(f32[6,2,8,128]{3,2,1,0:T(8,128)S(1)} %fusion.33), channel_id=1, source_target_pairs={{4,0},{8,4},{12,8},{0,12},{5,1},{9,5},{13,9},{1,13},{6,2},{10,6},{... | collective-permute-start | bytes 147464 | tf_op jit(solution)/shard_map/ppermute | solution.py:10
  47.2 7.1 %copy-start.8 = (s32[32]{0:T(128)S(1)}, s32[32]{0:T(128)}, u32[]{:S(2)}) copy-start(s32[32]{0:T(128)} %param.16) | copy-start | bytes 388
  47.2 5.1 %collective-permute-start.11 = (f32[6,2,8,128]{3,2,1,0:T(8,128)S(1)}, f32[6,2,8,128]{3,2,1,0:T(8,128)S(1)}, u32[]{:S(2)}, u32[]{:S(2)}) collective-permute-start(f32[6,2,8,128]{3,2,1,0:T(8,128)S(1)} %broadcast_select_fusion.2), channel_id=1, source_target_pairs={{8,0},{12,4},{0,8},{4,12},{9,1},{13,5},{1,9},{5,13},{10,2},{14,6},... | collective-permute-start | bytes 147464 | tf_op jit(solution)/shard_map/ppermute | solution.py:10
  52.2 4.1 %collective-permute-start.12 = (f32[6,2,8,128]{3,2,1,0:T(8,128)S(1)}, f32[6,2,8,128]{3,2,1,0:T(8,128)S(1)}, u32[]{:S(2)}, u32[]{:S(2)}) collective-permute-start(f32[6,2,8,128]{3,2,1,0:T(8,128)S(1)} %broadcast_select_fusion.6), channel_id=1, source_target_pairs={{4,0},{8,4},{12,8},{0,12},{5,1},{9,5},{13,9},{1,13},{6,2},{10,6},{... | collective-permute-start | bytes 147464 | tf_op jit(solution)/shard_map/ppermute | solution.py:10
  56.5 5.2 %collective-permute-start.13 = (f32[6,2,1,128]{3,2,1,0:T(1,128)S(1)}, f32[6,2,1,128]{3,2,1,0:T(1,128)S(1)}, u32[]{:S(2)}, u32[]{:S(2)}) collective-permute-start(f32[6,2,1,128]{3,2,1,0:T(1,128)S(1)} %get-tuple-element.17), channel_id=1, source_target_pairs={{4,0},{8,4},{12,8},{0,12},{5,1},{9,5},{13,9},{1,13},{6,2},{10,6},{... | collective-permute-start | bytes 18440 | tf_op jit(solution)/shard_map/ppermute | solution.py:21
  60.4 0.7 copy-start.2
  60.4 5.4 %collective-permute-start.14 = (f32[6,2,1,128]{3,2,1,0:T(1,128)S(1)}, f32[6,2,1,128]{3,2,1,0:T(1,128)S(1)}, u32[]{:S(2)}, u32[]{:S(2)}) collective-permute-start(f32[6,2,1,128]{3,2,1,0:T(1,128)S(1)} %get-tuple-element.18), channel_id=1, source_target_pairs={{0,4},{4,8},{8,12},{12,0},{1,5},{5,9},{9,13},{13,1},{2,6},{6,10},{... | collective-permute-start | bytes 18440 | tf_op jit(solution)/shard_map/ppermute | solution.py:20
  61.2 4.7 %copy-start.3 = (f32[8,128]{1,0:T(8,128)S(1)}, f32[8,128]{1,0:T(8,128)}, u32[]{:S(2)}) copy-start(f32[8,128]{1,0:T(8,128)} %param.14) | copy-start | bytes 12292
  61.2 4.7 %copy-start.7 = (s32[8,128]{1,0:T(8,128)S(1)}, s32[8,128]{1,0:T(8,128)}, u32[]{:S(2)}) copy-start(s32[8,128]{1,0:T(8,128)} %param.15) | copy-start | bytes 12292
  94.3 5.5 %collective-permute-start.15 = (f32[6,2,1,128]{3,2,1,0:T(1,128)S(1)}, f32[6,2,1,128]{3,2,1,0:T(1,128)S(1)}, u32[]{:S(2)}, u32[]{:S(2)}) collective-permute-start(f32[6,2,1,128]{3,2,1,0:T(1,128)S(1)} %get-tuple-element.27), channel_id=1, source_target_pairs={{0,4},{4,8},{8,12},{12,0},{1,5},{5,9},{9,13},{13,1},{2,6},{6,10},{... | collective-permute-start | bytes 18440 | tf_op jit(solution)/shard_map/ppermute | solution.py:20
  94.3 5.5 %collective-permute-start.16 = (f32[6,2,1,128]{3,2,1,0:T(1,128)S(1)}, f32[6,2,1,128]{3,2,1,0:T(1,128)S(1)}, u32[]{:S(2)}, u32[]{:S(2)}) collective-permute-start(f32[6,2,1,128]{3,2,1,0:T(1,128)S(1)} %get-tuple-element.28), channel_id=1, source_target_pairs={{4,0},{8,4},{12,8},{0,12},{5,1},{9,5},{13,9},{1,13},{6,2},{10,6},{... | collective-permute-start | bytes 18440 | tf_op jit(solution)/shard_map/ppermute | solution.py:21
  99.8 5.9 %collective-permute-start.17 = (f32[6,2,8,128]{3,2,1,0:T(8,128)S(1)}, f32[6,2,8,128]{3,2,1,0:T(8,128)S(1)}, u32[]{:S(2)}, u32[]{:S(2)}) collective-permute-start(f32[6,2,8,128]{3,2,1,0:T(8,128)S(1)} %fusion.28), channel_id=1, source_target_pairs={{12,0},{0,4},{4,8},{8,12},{13,1},{1,5},{5,9},{9,13},{14,2},{2,6},{... | collective-permute-start | bytes 147464 | tf_op jit(solution)/shard_map/ppermute | solution.py:10
  105.8 5.1 %collective-permute-start.18 = (f32[6,2,8,128]{3,2,1,0:T(8,128)S(1)}, f32[6,2,8,128]{3,2,1,0:T(8,128)S(1)}, u32[]{:S(2)}, u32[]{:S(2)}) collective-permute-start(f32[6,2,8,128]{3,2,1,0:T(8,128)S(1)} %broadcast_select_fusion.1), channel_id=1, source_target_pairs={{8,0},{12,4},{0,8},{4,12},{9,1},{13,5},{1,9},{5,13},{10,2},{14,6},... | collective-permute-start | bytes 147464 | tf_op jit(solution)/shard_map/ppermute | solution.py:10
  110.9 5.9 %collective-permute-start.19 = (f32[6,2,8,128]{3,2,1,0:T(8,128)S(1)}, f32[6,2,8,128]{3,2,1,0:T(8,128)S(1)}, u32[]{:S(2)}, u32[]{:S(2)}) collective-permute-start(f32[6,2,8,128]{3,2,1,0:T(8,128)S(1)} %broadcast_select_fusion.5), channel_id=1, source_target_pairs={{12,0},{0,4},{4,8},{8,12},{13,1},{1,5},{5,9},{9,13},{14,2},{2,6},{... | collective-permute-start | bytes 147464 | tf_op jit(solution)/shard_map/ppermute | solution.py:10
  117.0 4.3 %collective-permute-start.20 = (f32[6,2,8,1]{3,2,1,0:T(8,128)S(1)}, f32[6,2,8,1]{3,2,1,0:T(8,128)S(1)}, u32[]{:S(2)}, u32[]{:S(2)}) collective-permute-start(f32[6,2,8,1]{3,2,1,0:T(8,128)S(1)} %get-tuple-element.15), channel_id=1, source_target_pairs={{2,0},{3,1},{6,4},{7,5},{10,8},{11,9},{14,12},{15,13},{18,16},{19,... | collective-permute-start | bytes 1160 | tf_op jit(solution)/shard_map/ppermute | solution.py:21
  118.3 3.9 %collective-permute-start.21 = (f32[6,2,8,1]{3,2,1,0:T(8,128)S(1)}, f32[6,2,8,1]{3,2,1,0:T(8,128)S(1)}, u32[]{:S(2)}, u32[]{:S(2)}) collective-permute-start(f32[6,2,8,1]{3,2,1,0:T(8,128)S(1)} %get-tuple-element.16), channel_id=1, source_target_pairs={{0,2},{1,3},{4,6},{5,7},{8,10},{9,11},{12,14},{13,15},{16,18},{17,... | collective-permute-start | bytes 1160 | tf_op jit(solution)/shard_map/ppermute | solution.py:20
  122.3 5.5 %collective-permute-start.22 = (f32[6,2,1,128]{3,2,1,0:T(1,128)S(1)}, f32[6,2,1,128]{3,2,1,0:T(1,128)S(1)}, u32[]{:S(2)}, u32[]{:S(2)}) collective-permute-start(f32[6,2,1,128]{3,2,1,0:T(1,128)S(1)} %get-tuple-element.21), channel_id=1, source_target_pairs={{0,4},{4,8},{8,12},{12,0},{1,5},{5,9},{9,13},{13,1},{2,6},{6,10},{... | collective-permute-start | bytes 18440 | tf_op jit(solution)/shard_map/ppermute | solution.py:20
  122.4 5.4 %collective-permute-start.23 = (f32[6,2,1,128]{3,2,1,0:T(1,128)S(1)}, f32[6,2,1,128]{3,2,1,0:T(1,128)S(1)}, u32[]{:S(2)}, u32[]{:S(2)}) collective-permute-start(f32[6,2,1,128]{3,2,1,0:T(1,128)S(1)} %get-tuple-element.22), channel_id=1, source_target_pairs={{4,0},{8,4},{12,8},{0,12},{5,1},{9,5},{13,9},{1,13},{6,2},{10,6},{... | collective-permute-start | bytes 18440 | tf_op jit(solution)/shard_map/ppermute | solution.py:21
  127.9 6.0 %collective-permute-start.24 = (f32[6,2,8,128]{3,2,1,0:T(8,128)S(1)}, f32[6,2,8,128]{3,2,1,0:T(8,128)S(1)}, u32[]{:S(2)}, u32[]{:S(2)}) collective-permute-start(f32[6,2,8,128]{3,2,1,0:T(8,128)S(1)} %fusion.18), channel_id=1, source_target_pairs={{12,0},{0,4},{4,8},{8,12},{13,1},{1,5},{5,9},{9,13},{14,2},{2,6},{... | collective-permute-start | bytes 147464 | tf_op jit(solution)/shard_map/ppermute | solution.py:10
  134.0 5.1 %collective-permute-start.25 = (f32[6,2,8,128]{3,2,1,0:T(8,128)S(1)}, f32[6,2,8,128]{3,2,1,0:T(8,128)S(1)}, u32[]{:S(2)}, u32[]{:S(2)}) collective-permute-start(f32[6,2,8,128]{3,2,1,0:T(8,128)S(1)} %broadcast_select_fusion), channel_id=1, source_target_pairs={{8,0},{12,4},{0,8},{4,12},{9,1},{13,5},{1,9},{5,13},{10,2},{14,6},... | collective-permute-start | bytes 147464 | tf_op jit(solution)/shard_map/ppermute | solution.py:10
  139.0 5.9 %collective-permute-start.26 = (f32[6,2,8,128]{3,2,1,0:T(8,128)S(1)}, f32[6,2,8,128]{3,2,1,0:T(8,128)S(1)}, u32[]{:S(2)}, u32[]{:S(2)}) collective-permute-start(f32[6,2,8,128]{3,2,1,0:T(8,128)S(1)} %broadcast_select_fusion.4), channel_id=1, source_target_pairs={{12,0},{0,4},{4,8},{8,12},{13,1},{1,5},{5,9},{9,13},{14,2},{2,6},{... | collective-permute-start | bytes 147464 | tf_op jit(solution)/shard_map/ppermute | solution.py:10
  145.1 4.3 %collective-permute-start.27 = (f32[6,2,8,1]{3,2,1,0:T(8,128)S(1)}, f32[6,2,8,1]{3,2,1,0:T(8,128)S(1)}, u32[]{:S(2)}, u32[]{:S(2)}) collective-permute-start(f32[6,2,8,1]{3,2,1,0:T(8,128)S(1)} %get-tuple-element.13), channel_id=1, source_target_pairs={{2,0},{3,1},{6,4},{7,5},{10,8},{11,9},{14,12},{15,13},{18,16},{19,... | collective-permute-start | bytes 1160 | tf_op jit(solution)/shard_map/ppermute | solution.py:21
  146.4 3.9 %collective-permute-start.28 = (f32[6,2,8,1]{3,2,1,0:T(8,128)S(1)}, f32[6,2,8,1]{3,2,1,0:T(8,128)S(1)}, u32[]{:S(2)}, u32[]{:S(2)}) collective-permute-start(f32[6,2,8,1]{3,2,1,0:T(8,128)S(1)} %get-tuple-element.14), channel_id=1, source_target_pairs={{0,2},{1,3},{4,6},{5,7},{8,10},{9,11},{12,14},{13,15},{16,18},{17,... | collective-permute-start | bytes 1160 | tf_op jit(solution)/shard_map/ppermute | solution.py:20
where the time goes:
time: 152 us; the launch traced here: 151 us
  waiting for transfers between devices  68.3 us (45%)
  starting transfers between devices  48.4 us (32%)
  blocking collectives  25.9 us (17%)
  other arithmetic  3.48 us (2%)
  local copies, waits for them, and re-layouts  3.17 us (2%)
    ppermute x12, waiting for transfers between devices, from_behind(): return lax.ppermute(block, axis, route)  51.7 us
    psum x1, blocking collectives, on_device(): scaled = lax.psum(slot_sums, ('lon', 'lat')) * prior_slot  25.9 us
    ppermute x8, starting transfers between devices, extended(): after = lax.ppermute(first, axis, down)  20.9 us
    ppermute x8, waiting for transfers between devices, extended(): before = lax.ppermute(last, axis, up)  14.7 us
    ppermute x12, starting transfers between devices, from_behind(): return lax.ppermute(block, axis, route)  12.8 us
    ppermute x8, starting transfers between devices, extended(): before = lax.ppermute(last, axis, up)  12.2 us
  transfers between devices with their start and end apart: 29, of which 22 were waited for; matrix products, arithmetic and copies ran while one was open for 1% of the time, Pallas kernels for 0%

commit v1 on v0

v1 whole, which is shorter than its diff:
```python
import functools

import jax
import jax.numpy as jnp
from jax import lax
from jax.experimental import pallas as pl
from jax.experimental.pallas import tpu as pltpu
from jax.sharding import PartitionSpec as P

SUB, LANES = 8, 128


def swapped(block, axis, k):
    size = lax.axis_size(axis)
    return lax.ppermute(block, axis, [(i, i ^ k) for i in range(size)])


def transport_kernel(tracers, blocks, regions, own_ref, other_ref, owner_ref, prior_ref, out_ref, flat_ref):
    f32, i32 = jnp.float32, jnp.int32
    me = lax.axis_index("lon")
    place = [me ^ ((me + b) % blocks) if b else 0 for b in range(blocks)]
    bands = (own_ref, other_ref)
    cycle = blocks * SUB
    row = lax.broadcasted_iota(i32, (SUB, LANES), 0)
    lane = lax.broadcasted_iota(i32, (SUB, LANES), 1)
    first_row, last_row = row == 0, row == SUB - 1
    first_lane, last_lane = lane == 0, lane == LANES - 1
    base = tracers * 2 * SUB

    def tile(h, b, at):
        return bands[h][place[b], at : at + SUB, :]

    def full(h, at):
        return jnp.broadcast_to(bands[h][0, at : at + 1, :], (SUB, LANES))

    foot = [[tile(h, b, base) for h in range(2)] for b in range(blocks)]
    region = [[tile(h, b, base + SUB).astype(i32) for h in range(2)] for b in range(blocks)]
    half = [[0.5 * tile(h, b, base + 2 * SUB) for h in range(2)] for b in range(blocks)]
    at = base + 3 * SUB
    shift = [[full(h, at + l).astype(i32) for h in range(2)] for l in range(2)]
    frac = [[full(h, at + 2 + l) for h in range(2)] for l in range(2)]
    face = [[full(h, at + 4 + l) for h in range(2)] for l in range(2)]
    w_left = [[a * (a + 1.0) * 0.5 for a in x] for x in frac]
    w_centre = [[1.0 - a * a for a in x] for x in frac]
    w_right = [[a * (a - 1.0) * 0.5 for a in x] for x in frac]

    def north(v):
        r = [pltpu.roll(x, LANES - 1, 1) for x in v]
        return [jnp.where(last_lane, r[1], r[0]), jnp.where(last_lane, r[0], r[1])]

    def south(v):
        r = [pltpu.roll(x, 1, 1) for x in v]
        return [jnp.where(first_lane, r[1], r[0]), jnp.where(first_lane, r[0], r[1])]

    face_prev = [south(x) for x in face]
    face_mid = [[1.0 - face[l][h] - face_prev[l][h] for h in range(2)] for l in range(2)]

    def meridional(v, l, only=(0, 1)):
        n, s = north(v), south(v)
        return [face_mid[l][h] * v[h] + face[l][h] * n[h] + face_prev[l][h] * s[h] for h in only]

    def mod(e):
        return jnp.where(e >= blocks, e - blocks, e)

    steps = range((blocks - 1).bit_length())

    def bits(e):
        return [(e >> k) & 1 == 1 for k in steps]

    def plan(amount, ahead):
        whole, within = amount >> 3, amount & 7
        if ahead:
            crossed = (row < within).astype(i32)
            index = (row + within) & 7
        else:
            crossed = (row + within >= SUB).astype(i32)
            index = (row - within) & 7
        return bits(mod(mod(whole + crossed))), index

    def pick(v, plan, sign, wanted):
        masks, index = plan
        need = list(wanted)
        chain = []
        for k in reversed(steps):
            chain.append(need)
            need = sorted({(b + d) % blocks for b in need for d in (0, sign << k)})
        current = {b: v[b] for b in need}
        for k, need in zip(steps, reversed(chain)):
            current = {b: jnp.where(masks[k], current[(b + (sign << k)) % blocks], current[b]) for b in need}
        return [jnp.take_along_axis(current[b], index, axis=0, mode="promise_in_bounds") for b in wanted]

    def beside(v):
        up = [pltpu.roll(x, SUB - 1, 0) for x in v]
        down = [pltpu.roll(x, 1, 0) for x in v]
        after = [jnp.where(last_row, up[(b + 1) % blocks], up[b]) for b in range(blocks)]
        before = [jnp.where(first_row, down[(b - 1) % blocks], down[b]) for b in range(blocks)]
        return before, after

    every = range(blocks)
    plan_adjoint = [[plan(shift[l][h], True) for h in range(2)] for l in range(2)]
    plan_first = [plan(shift[0][h], False) for h in range(2)]
    plan_second = [
        [[plan(shift[l][h] + d, False) for d in (1, 0, -1)] for h in range(2)] for l in range(2)
    ]

    def zonal_adjoint(v, l):
        result = []
        for h in range(2):
            q = pick([v[b][h] for b in every], plan_adjoint[l][h], 1, every)
            before, after = beside(q)
            result.append(
                [w_left[l][h] * after[b] + w_centre[l][h] * q[b] + w_right[l][h] * before[b] for b in every]
            )
        return [[result[h][b] for h in range(2)] for b in every]

    for t in range(tracers):
        v = [[[tile(h, b, (2 * t + l) * SUB) for h in range(2)] for b in every] for l in range(2)]
        mixed = [[], []]
        for b in every:
            d = [half[b][h] * (v[1][b][h] - v[0][b][h]) for h in range(2)]
            mixed[0].append(meridional([v[0][b][h] + d[h] for h in range(2)], 0))
            mixed[1].append(meridional([v[1][b][h] - d[h] for h in range(2)], 1))
        v = [zonal_adjoint(mixed[l], l) for l in range(2)]
        mixed = [
            meridional([v[0][b][h] + half[b][h] * (v[1][b][h] - v[0][b][h]) for h in range(2)], 0) for b in every
        ]
        v = zonal_adjoint(mixed, 0)
        for b in every:
            for h in range(2):
                flat_ref[b, t * SUB : (t + 1) * SUB, h * LANES : (h + 1) * LANES] = foot[b][h] * v[b][h]

    bf16 = jnp.bfloat16
    lines = tracers * SUB
    total = jnp.zeros((3 * lines, SUB * regions), f32)
    number = lax.broadcasted_iota(i32, (1, regions, 2 * LANES), 1)
    for b in every:
        x = flat_ref[b]
        hi = x.astype(bf16)
        rest = x - hi.astype(f32)
        mid = rest.astype(bf16)
        low = (rest - mid.astype(f32)).astype(bf16)
        ids = jnp.concatenate(region[b], axis=1)
        same = ids[:, None, :] == number
        table = jnp.where(same, 1.0, 0.0).astype(bf16).reshape(SUB * regions, 2 * LANES)
        total = total + lax.dot_general(
            jnp.concatenate([hi, mid, low], axis=0),
            table,
            (((1,), (1,)), ((), ())),
            preferred_element_type=f32,
        )
    sums = total[:lines] + total[lines : 2 * lines] + total[2 * lines :]
    width = SUB * regions
    column = lax.broadcasted_iota(i32, (SUB, width), 1)
    keep = column // regions == lax.broadcasted_iota(i32, (SUB, width), 0)
    sums = jnp.concatenate(
        [
            jnp.sum(jnp.where(keep, sums[t * SUB : (t + 1) * SUB], 0.0), axis=0, keepdims=True)
            for t in range(tracers)
        ],
        axis=0,
    )
    while width > max(regions, LANES):
        width //= 2
        sums = sums[:, :width] + sums[:, width:]
    period = width
    while period > regions:
        period //= 2
        sums = sums + pltpu.roll(sums, period, 1)
    spot = lax.broadcasted_iota(i32, (width, regions), 0) % regions
    holds = jnp.where(spot == owner_ref[...], 1.0, 0.0)
    prior = lax.dot_general(
        prior_ref[...],
        holds,
        (((1,), (1,)), ((), ())),
        precision=lax.Precision.HIGHEST,
        preferred_element_type=f32,
    )
    scaled = sums * prior

    keep0 = [[1.0 - x for x in y] for y in half]
    for t in range(tracers):
        rows = jnp.broadcast_to(scaled[t : t + 1], (SUB, width))

        def spread(ids):
            result = None
            for k in range(width // LANES):
                part = jnp.take_along_axis(
                    rows[:, k * LANES : (k + 1) * LANES], ids & (LANES - 1), axis=1, mode="promise_in_bounds"
                )
                result = part if k == 0 else jnp.where(ids >> 7 == k, part, result)
            return result

        v = [[foot[b][h] * spread(region[b][h]) for h in range(2)] for b in every]
        u = []
        for h in range(2):
            p = pick([v[b][h] for b in every], plan_first[h], -1, every)
            before, after = beside(p)
            u.append(
                [w_left[0][h] * before[b] + w_centre[0][h] * p[b] + w_right[0][h] * after[b] for b in every]
            )
        u = [meridional([u[h][b] for h in range(2)], 0) for b in every]
        pair = [
            [[keep0[b][h] * u[b][h] for h in range(2)] for b in every],
            [[half[b][h] * u[b][h] for h in range(2)] for b in every],
        ]
        moved = []
        for l in range(2):
            z = []
            for h in range(2):
                source = [pair[l][b][h] for b in every]
                before, centre, after = (pick(source, p, -1, [0])[0] for p in plan_second[l][h])
                z.append(w_left[l][h] * before + w_centre[l][h] * centre + w_right[l][h] * after)
            moved.append(meridional(z, l, (0,))[0])
        d = half[0][0] * (moved[1] - moved[0])
        out_ref[t, 0] = tile(0, 0, 2 * t * SUB) * (moved[0] + d)
        out_ref[t, 1] = tile(0, 0, (2 * t + 1) * SUB) * (moved[1] - d)


def on_device(
    probe_signs,
    shift_cells,
    courant_frac,
    merid_coef,
    convect_frac,
    footprint,
    region_id,
    owner_slots,
    prior_slot,
):
    tracers, levels, width, rows = probe_signs.shape
    blocks, bands = lax.axis_size("lon"), lax.axis_size("lat")
    assert (levels, width, rows, bands) == (2, SUB, LANES, 2) and blocks & (blocks - 1) == 0
    regions = owner_slots.shape[0]
    f32 = jnp.float32
    at = lax.axis_index("lat") * rows + jnp.arange(rows, dtype=jnp.int32)
    faces = jnp.where((at == bands * rows - 1)[None, :], 0.0, merid_coef)
    block = jnp.concatenate(
        [
            (2 * probe_signs - 1).astype(f32).reshape(tracers * levels * width, rows),
            footprint,
            region_id.astype(f32),
            convect_frac,
            shift_cells.astype(f32),
            courant_frac,
            faces,
            jnp.zeros((2, rows), f32),
        ],
        axis=0,
    )
    own = jnp.stack([block] + [swapped(block, "lon", k) for k in range(1, blocks)])
    other = swapped(own, "lat", 1)
    return pl.pallas_call(
        functools.partial(transport_kernel, tracers, blocks, regions),
        out_shape=jax.ShapeDtypeStruct(probe_signs.shape, f32),
        in_specs=[pl.BlockSpec(memory_space=pltpu.VMEM)] * 4,
        out_specs=pl.BlockSpec(memory_space=pltpu.VMEM),
        scratch_shapes=[pltpu.VMEM((blocks, tracers * SUB, 2 * LANES), f32)],
        compiler_params=pltpu.CompilerParams(vmem_limit_bytes=48 * 1024 * 1024),
    )(own, other, owner_slots.reshape(1, regions), prior_slot)


def solution(mesh):
    placed = (
        P(("probe", "trc"), None, "lon", "lat"),
        P(None, "lat"),
        P(None, "lat"),
        P(None, "lat"),
        P("lon", "lat"),
        P("lon", "lat"),
        P("lon", "lat"),
        P(),
        P("trc", None),
    )
    return jax.shard_map(
        on_device,
        mesh=mesh,
        in_specs=placed,
        out_specs=P(("probe", "trc"), None, "lon", "lat"),
        check_vma=False,
    )
```

time: 152 us -> 17 us (0.11)
  waiting for transfers between devices: 68.3 us -> 6.48 us
  starting transfers between devices: 48.4 us -> 5.82 us
  blocking collectives: 25.9 us -> 0 us
  other arithmetic: 3.48 us -> 0.85 us
  Pallas kernels: 0 us -> 2.17 us
  local copies, waits for them, and re-layouts: 3.17 us -> 1.39 us
    ppermute x29 -> x4, waiting for transfers between devices: 68.3 us -> 6.48 us  [swapped(): return lax.ppermute(block, axis, [(i, i ^ k) for i in range(size)])]
    ppermute x29 -> x4, starting transfers between devices: 48.4 us -> 5.82 us  [swapped(): return lax.ppermute(block, axis, [(i, i ^ k) for i in range(size)])]
    psum x1 -> x0, blocking collectives: 25.9 us -> none  [on_device(): scaled = lax.psum(slot_sums, ('lon', 'lat')) * prior_slot]
    pallas_call x0 -> x1, Pallas kernels: none -> 2.17 us  [on_device(): pl.pallas_call(functools.partial(transport_kernel, tracers, blocks, regio...]
  transfers between devices with their start and end apart: 29 -> 4, of which waited for: 22 -> 3; matrix products, arithmetic and copies ran while one was open for 1% -> 0% of each run, Pallas kernels for 0% -> 0%
where the time goes in v1:
time: 17 us; the launch traced here: 16.8 us
  waiting for transfers between devices  6.48 us (38%)
  starting transfers between devices  5.82 us (34%)
  Pallas kernels  2.17 us (13%)
  local copies, waits for them, and re-layouts  1.39 us (8%)
  other arithmetic  0.85 us (5%)
    ppermute x4, waiting for transfers between devices, swapped(): return lax.ppermute(block, axis, [(i, i ^ k) for i in range(size)])  6.48 us
    ppermute x4, starting transfers between devices, swapped(): return lax.ppermute(block, axis, [(i, i ^ k) for i in range(size)])  5.82 us
    pallas_call x1, Pallas kernels, on_device(): pl.pallas_call(functools.partial(transport_kernel, tracers, blocks, regio...  2.17 us
    unnamed x16, local copies, waits for them, and re-layouts  1.37 us
    convert_element_type x1, other arithmetic, on_device(): (2 * probe_signs - 1).astype(f32).reshape(tracers * levels * width, rows)  0.82 us
  transfers between devices with their start and end apart: 4, of which 3 were waited for; matrix products, arithmetic and copies ran while one was open for 0% of the time, Pallas kernels for 0%

profile of v1, /device:TPU:0, one launch (start us, length us, event | category | flops | bytes accessed | tf_op | source)
XLA Modules:
  0.0 16.8 jit_solution(12858760637372082535)
XLA Ops:
  0.0 0.0 copy-start.4
  0.0 0.0 copy-start.6
  0.0 0.7 %copy-done.6 = s32[2,128]{1,0:T(2,128)S(1)} copy-done((s32[2,128]{1,0:T(2,128)S(1)}, s32[2,128]{1,0:T(2,128)}, u32[]{:S(2)}) %copy-start.6) | copy-done | bytes 1048
  0.7 0.0 copy-done.4
  0.7 0.0 copy-start.7
  0.7 0.0 copy-start.3
  0.7 0.8 %add_convert_fusion = f32[6,2,8,128]{3,2,1,0:T(8,128)S(1)} fusion(s32[6,2,8,128]{3,2,1,0:T(8,128)} %param.9), kind=kLoop, calls=%fused_computation.1 | loop fusion | flops 36864 | bytes 98304 | tf_op jit(solution)/shard_map/convert_element_type | solution.py:239
  1.5 0.0 copy-done.7
  1.5 0.0 copy-start.2
  1.6 0.0 copy-start.5
  1.6 0.0 copy-done.3
  1.6 0.6 %copy-done.2 = f32[8,128]{1,0:T(8,128)S(1)} copy-done((f32[8,128]{1,0:T(8,128)S(1)}, f32[8,128]{1,0:T(8,128)}, u32[]{:S(2)}) %copy-start.2) | copy-done | bytes 4120
  2.2 0.0 copy-done.5
  2.3 5.1 %collective-permute-start.2 = (f32[128,128]{1,0:T(8,128)S(1)}, f32[128,128]{1,0:T(8,128)S(1)}, u32[]{:S(2)}, u32[]{:S(2)}) collective-permute-start(f32[128,128]{1,0:T(8,128)S(1)} %concatenate.3), channel_id=1, source_target_pairs={{0,12},{4,8},{8,4},{12,0},{1,13},{5,9},{9,5},{13,1},{2,14},{6,10},... | collective-permute-start | bytes 196616 | tf_op jit(solution)/shard_map/ppermute | solution.py:15
  7.4 0.0 collective-permute-start.1
  7.4 0.6 %collective-permute-start = (f32[128,128]{1,0:T(8,128)S(1)}, f32[128,128]{1,0:T(8,128)S(1)}, u32[]{:S(2)}, u32[]{:S(2)}) collective-permute-start(f32[128,128]{1,0:T(8,128)S(1)} %concatenate.3), channel_id=1, source_target_pairs={{0,4},{4,0},{8,12},{12,8},{1,5},{5,1},{9,13},{13,9},{2,6},{6,2},{1... | collective-permute-start | bytes 196616 | tf_op jit(solution)/shard_map/ppermute | solution.py:15
  8.0 1.9 %collective-permute-done.2 = f32[128,128]{1,0:T(8,128)S(1)} collective-permute-done((f32[128,128]{1,0:T(8,128)S(1)}, f32[128,128]{1,0:T(8,128)S(1)}, u32[]{:S(2)}, u32[]{:S(2)}) %collective-permute-start.2) | collective-permute-done | bytes 65568 | tf_op jit(solution)/shard_map/ppermute | solution.py:15
  10.0 3.0 %collective-permute-done.1 = f32[128,128]{1,0:T(8,128)S(1)} collective-permute-done((f32[128,128]{1,0:T(8,128)S(1)}, f32[128,128]{1,0:T(8,128)S(1)}, u32[]{:S(2)}, u32[]{:S(2)}) %collective-permute-start.1) | collective-permute-done | bytes 65568 | tf_op jit(solution)/shard_map/ppermute | solution.py:15
  13.0 0.0 collective-permute-done
  13.0 0.0 copy-start
  13.0 0.0 copy-start.1
  13.0 0.1 collective-permute-start.3
  13.1 1.5 %collective-permute-done.3.other_ref = f32[4,128,128]{2,1,0:T(8,128)S(1)} collective-permute-done((f32[4,128,128]{2,1,0:T(8,128)S(1)}, f32[4,128,128]{2,1,0:T(8,128)S(1)}, u32[]{:S(2)}, u32[]{:S(2)}) %collective-permute-start.3) | collective-permute-done | bytes 262176 | tf_op jit(solution)/shard_map/ppermute | solution.py:15
  14.6 0.0 copy-done
  14.6 0.0 copy-done.1
  14.6 2.2 %shard_map.91 = f32[6,2,8,128]{3,2,1,0:T(8,128)} custom-call(f32[4,128,128]{2,1,0:T(8,128)S(1)} %pad_maximum_fusion.own_ref, f32[4,128,128]{2,1,0:T(8,128)S(1)} %collective-permute-done.3.other_ref, s32[1,32]{1,0:T(1,128)S(1)} %bitcast.6, f32[6,32]{1,0:T(8,128)S(1)} %copy-done), custom_call_target="tpu_custom_call" | custom-call | tf_op jit(solution)/shard_map/pallas_call | solution.py:252
  (7 shorter events, 0.1 us)
Async XLA Ops:
  0.0 0.7 %copy-start.4 = (s32[8,128]{1,0:T(8,128)S(1)}, s32[8,128]{1,0:T(8,128)}, u32[]{:S(2)}) copy-start(s32[8,128]{1,0:T(8,128)} %param.15) | copy-start | bytes 12292
  0.0 0.7 %copy-start.6 = (s32[2,128]{1,0:T(2,128)S(1)}, s32[2,128]{1,0:T(2,128)}, u32[]{:S(2)}) copy-start(s32[2,128]{1,0:T(2,128)} %param.10) | copy-start | bytes 3076
  0.7 0.8 %copy-start.7 = (f32[2,128]{1,0:T(2,128)S(1)}, f32[2,128]{1,0:T(2,128)}, u32[]{:S(2)}) copy-start(f32[2,128]{1,0:T(2,128)} %param.12) | copy-start | bytes 3076
  0.7 0.9 %copy-start.3 = (f32[8,128]{1,0:T(8,128)S(1)}, f32[8,128]{1,0:T(8,128)}, u32[]{:S(2)}) copy-start(f32[8,128]{1,0:T(8,128)} %param.13) | copy-start | bytes 12292
  1.5 0.7 %copy-start.2 = (f32[8,128]{1,0:T(8,128)S(1)}, f32[8,128]{1,0:T(8,128)}, u32[]{:S(2)}) copy-start(f32[8,128]{1,0:T(8,128)} %param.14) | copy-start | bytes 12292
  1.6 0.7 %copy-start.5 = (f32[2,128]{1,0:T(2,128)S(1)}, f32[2,128]{1,0:T(2,128)}, u32[]{:S(2)}) copy-start(f32[2,128]{1,0:T(2,128)} %param.11) | copy-start | bytes 3076
  2.3 7.7 %collective-permute-start.2 = (f32[128,128]{1,0:T(8,128)S(1)}, f32[128,128]{1,0:T(8,128)S(1)}, u32[]{:S(2)}, u32[]{:S(2)}) collective-permute-start(f32[128,128]{1,0:T(8,128)S(1)} %concatenate.3), channel_id=1, source_target_pairs={{0,12},{4,8},{8,4},{12,0},{1,13},{5,9},{9,5},{13,1},{2,14},{6,10},... | collective-permute-start | bytes 196616 | tf_op jit(solution)/shard_map/ppermute | solution.py:15
  7.4 5.6 %collective-permute-start.1 = (f32[128,128]{1,0:T(8,128)S(1)}, f32[128,128]{1,0:T(8,128)S(1)}, u32[]{:S(2)}, u32[]{:S(2)}) collective-permute-start(f32[128,128]{1,0:T(8,128)S(1)} %concatenate.3), channel_id=1, source_target_pairs={{0,8},{4,12},{8,0},{12,4},{1,9},{5,13},{9,1},{13,5},{2,10},{6,14},... | collective-permute-start | bytes 196616 | tf_op jit(solution)/shard_map/ppermute | solution.py:15
  7.4 5.6 %collective-permute-start = (f32[128,128]{1,0:T(8,128)S(1)}, f32[128,128]{1,0:T(8,128)S(1)}, u32[]{:S(2)}, u32[]{:S(2)}) collective-permute-start(f32[128,128]{1,0:T(8,128)S(1)} %concatenate.3), channel_id=1, source_target_pairs={{0,4},{4,0},{8,12},{12,8},{1,5},{5,1},{9,13},{13,9},{2,6},{6,2},{1... | collective-permute-start | bytes 196616 | tf_op jit(solution)/shard_map/ppermute | solution.py:15
  13.0 1.6 %copy-start = (f32[6,32]{1,0:T(8,128)S(1)}, f32[6,32]{1,0:T(8,128)}, u32[]{:S(2)}) copy-start(f32[6,32]{1,0:T(8,128)} %prior_ref.1) | copy-start | bytes 2308
  13.0 1.6 %copy-start.1 = (s32[32]{0:T(128)S(1)}, s32[32]{0:T(128)}, u32[]{:S(2)}) copy-start(s32[32]{0:T(128)} %param.16) | copy-start | bytes 388
  13.0 1.6 %collective-permute-start.3 = (f32[4,128,128]{2,1,0:T(8,128)S(1)}, f32[4,128,128]{2,1,0:T(8,128)S(1)}, u32[]{:S(2)}, u32[]{:S(2)}) collective-permute-start(f32[4,128,128]{2,1,0:T(8,128)S(1)} %pad_maximum_fusion.own_ref), channel_id=1, source_target_pairs={{0,2},{2,0},{1,3},{3,1},{4,6},{6,4},{5,7},{7,5},{8,10},{10,8},{9,1... | collective-permute-start | bytes 786440 | tf_op jit(solution)/shard_map/ppermute | solution.py:15

commit v2 on v1

--- a/solution.py
+++ b/solution.py
@@ -15,10 +15,14 @@
     return lax.ppermute(block, axis, [(i, i ^ k) for i in range(size)])
 
 
+def slot_of(k, blocks):
+    return jnp.where(k > 1, blocks + 1 - k, k)
+
+
 def transport_kernel(tracers, blocks, regions, own_ref, other_ref, owner_ref, prior_ref, out_ref, flat_ref):
     f32, i32 = jnp.float32, jnp.int32
     me = lax.axis_index("lon")
-    place = [me ^ ((me + b) % blocks) if b else 0 for b in range(blocks)]
+    place = [slot_of(me ^ ((me + b) % blocks), blocks) if b else 0 for b in range(blocks)]
     bands = (own_ref, other_ref)
     cycle = blocks * SUB
     row = lax.broadcasted_iota(i32, (SUB, LANES), 0)
@@ -216,6 +220,41 @@
         out_ref[t, 1] = tile(0, 0, (2 * t + 1) * SUB) * (moved[1] - d)
 
 
+def pack_kernel(tracers, sign_ref, shift_ref, frac_ref, face_ref, convect_ref, foot_ref, region_ref, out_ref, *scratch):
+    f32, i32 = jnp.float32, jnp.int32
+    sources = (sign_ref, foot_ref, region_ref, convect_ref, shift_ref, frac_ref, face_ref)
+    held, arrived = scratch[:-1], scratch[-1]
+    copies = [
+        pltpu.make_async_copy(source, slot, arrived.at[n])
+        for n, (source, slot) in enumerate(zip(sources, held))
+    ]
+    for copy in copies:
+        copy.start()
+    signs, foot, region, convect, shift, frac, face = held
+    base = tracers * 2 * SUB
+    for n, slot in ((1, foot), (2, region), (3, convect)):
+        copies[n].wait()
+        out_ref[base + (n - 1) * SUB : base + n * SUB, :] = slot[...].astype(f32)
+    for n in (4, 5, 6):
+        copies[n].wait()
+    ends = lax.axis_index("lat") == lax.axis_size("lat") - 1
+    lane = lax.broadcasted_iota(i32, (2, LANES), 1)
+    closed = jnp.where(ends, LANES - 1, LANES)
+    out_ref[base + 3 * SUB : base + 4 * SUB, :] = jnp.concatenate(
+        [
+            shift[...].astype(f32),
+            frac[...],
+            jnp.where(lane == closed, 0.0, face[...]),
+            jnp.zeros((2, LANES), f32),
+        ],
+        axis=0,
+    )
+    copies[0].wait()
+    for t in range(tracers):
+        for l in range(2):
+            out_ref[(2 * t + l) * SUB : (2 * t + l + 1) * SUB, :] = (2 * signs[t, l] - 1).astype(f32)
+
+
 def on_device(
     probe_signs,
     shift_cells,
@@ -232,22 +271,17 @@
     assert (levels, width, rows, bands) == (2, SUB, LANES, 2) and blocks & (blocks - 1) == 0
     regions = owner_slots.shape[0]
     f32 = jnp.float32
-    at = lax.axis_index("lat") * rows + jnp.arange(rows, dtype=jnp.int32)
-    faces = jnp.where((at == bands * rows - 1)[None, :], 0.0, merid_coef)
-    block = jnp.concatenate(
-        [
-            (2 * probe_signs - 1).astype(f32).reshape(tracers * levels * width, rows),
-            footprint,
-            region_id.astype(f32),
-            convect_frac,
-            shift_cells.astype(f32),
-            courant_frac,
-            faces,
-            jnp.zeros((2, rows), f32),
-        ],
-        axis=0,
-    )
-    own = jnp.stack([block] + [swapped(block, "lon", k) for k in range(1, blocks)])
+    anywhere = pl.BlockSpec(memory_space=pl.ANY)
+    fields = (probe_signs, footprint, region_id, convect_frac, shift_cells, courant_frac, merid_coef)
+    block = pl.pallas_call(
+        functools.partial(pack_kernel, tracers),
+        out_shape=pltpu.VMEM((tracers * levels * width + 4 * SUB, rows), f32),
+        in_specs=[anywhere] * 7,
+        out_specs=pl.BlockSpec(memory_space=pltpu.VMEM),
+        scratch_shapes=[pltpu.VMEM(x.shape, x.dtype) for x in fields] + [pltpu.SemaphoreType.DMA((7,))],
+    )(probe_signs, shift_cells, courant_frac, merid_coef, convect_frac, footprint, region_id)
+    order = sorted(range(1, blocks), key=lambda k: (k > 1, -k))
+    own = jnp.stack([block] + [swapped(block, "lon", k) for k in order])
     other = swapped(own, "lat", 1)
     return pl.pallas_call(
         functools.partial(transport_kernel, tracers, blocks, regions),

time: 17 us -> 15.3 us (0.900)
  local copies, waits for them, and re-layouts: 1.39 us -> 0.01 us
  Pallas kernels: 2.17 us -> 3.05 us
  other arithmetic: 0.85 us -> 0.02 us
  waiting for transfers between devices: 6.48 us -> 6.26 us
    unnamed x16 -> x4, local copies, waits for them, and re-layouts: 1.37 us -> 0.01 us
    pallas_call x0 -> x1, Pallas kernels: none -> 0.87 us  [on_device(): pl.pallas_call(functools.partial(pack_kernel, tracers), out_shape=pltpu.V...]
    convert_element_type x3 -> x0, other arithmetic: 0.82 us -> none  [the longest x1 0.82 us: on_device(): (2 * probe_signs - 1).astype(f32).reshape(tracers * levels * width, rows)]
    ppermute x4, waiting for transfers between devices: 6.48 us -> 6.26 us  [swapped(): return lax.ppermute(block, axis, [(i, i ^ k) for i in range(size)])]
  transfers between devices with their start and end apart: 4 -> 4, of which waited for: 3 -> 4; matrix products, arithmetic and copies ran while one was open for 0% -> 0% of each run, Pallas kernels for 0% -> 0%
where the time goes in v2:
time: 15.3 us; the launch traced here: 15.1 us
  waiting for transfers between devices  6.26 us (41%)
  starting transfers between devices  5.75 us (38%)
  Pallas kernels  3.05 us (20%)
    ppermute x4, waiting for transfers between devices, swapped(): return lax.ppermute(block, axis, [(i, i ^ k) for i in range(size)])  6.26 us
    ppermute x4, starting transfers between devices, swapped(): return lax.ppermute(block, axis, [(i, i ^ k) for i in range(size)])  5.75 us
    pallas_call x1, Pallas kernels, on_device(): pl.pallas_call(functools.partial(transport_kernel, tracers, blocks, regio...  2.18 us
    pallas_call x1, Pallas kernels, on_device(): pl.pallas_call(functools.partial(pack_kernel, tracers), out_shape=pltpu.V...  0.87 us
  transfers between devices with their start and end apart: 4, of which 4 were waited for; matrix products, arithmetic and copies ran while one was open for 0% of the time, Pallas kernels for 0%

profile of v2, /device:TPU:0, one launch (start us, length us, event | category | flops | bytes accessed | tf_op | source)
XLA Modules:
  0.0 15.1 jit_solution(10742866958244168272)
XLA Ops:
  0.0 0.9 %shard_map.91 = f32[128,128]{1,0:T(8,128)S(1)} custom-call(s32[6,2,8,128]{3,2,1,0:T(8,128)} %sign_ref.1, s32[2,128]{1,0:T(2,128)} %shift_ref.1, f32[2,128]{1,0:T(2,128)} %frac_ref.1, f32[2,128]{1,0:T(2,128)} %face_ref.1, f32[8,128]{1,0:T(8,128)} %convect_ref.1, f32[8,128]{1,0:T(8,128)} %foot_ref.1, s32[8,128]{1,0:T(8,128)} %region_ref.1), custom_call_target="tpu_custom_call" | custom-call | tf_op jit(solution)/shard_map/pallas_call | solution.py:276
  0.9 4.1 %collective-permute-start.2 = (f32[128,128]{1,0:T(8,128)S(1)}, f32[128,128]{1,0:T(8,128)S(1)}, u32[]{:S(2)}, u32[]{:S(2)}) collective-permute-start(f32[128,128]{1,0:T(8,128)S(1)} %shard_map.91), channel_id=1, source_target_pairs={{0,8},{4,12},{8,0},{12,4},{1,9},{5,13},{9,1},{13,5},{2,10},{6,14},... | collective-permute-start | bytes 196616 | tf_op jit(solution)/shard_map/ppermute | solution.py:15
  5.0 1.3 %collective-permute-start.1 = (f32[128,128]{1,0:T(8,128)S(1)}, f32[128,128]{1,0:T(8,128)S(1)}, u32[]{:S(2)}, u32[]{:S(2)}) collective-permute-start(f32[128,128]{1,0:T(8,128)S(1)} %shard_map.91), channel_id=1, source_target_pairs={{0,12},{4,8},{8,4},{12,0},{1,13},{5,9},{9,5},{13,1},{2,14},{6,10},... | collective-permute-start | bytes 196616 | tf_op jit(solution)/shard_map/ppermute | solution.py:15
  6.3 0.2 %collective-permute-start = (f32[128,128]{1,0:T(8,128)S(1)}, f32[128,128]{1,0:T(8,128)S(1)}, u32[]{:S(2)}, u32[]{:S(2)}) collective-permute-start(f32[128,128]{1,0:T(8,128)S(1)} %shard_map.91), channel_id=1, source_target_pairs={{0,4},{4,0},{8,12},{12,8},{1,5},{5,1},{9,13},{13,9},{2,6},{6,2},{1... | collective-permute-start | bytes 196616 | tf_op jit(solution)/shard_map/ppermute | solution.py:15
  6.6 2.2 %collective-permute-done.2 = f32[128,128]{1,0:T(8,128)S(1)} collective-permute-done((f32[128,128]{1,0:T(8,128)S(1)}, f32[128,128]{1,0:T(8,128)S(1)}, u32[]{:S(2)}, u32[]{:S(2)}) %collective-permute-start.2) | collective-permute-done | bytes 65568 | tf_op jit(solution)/shard_map/ppermute | solution.py:15
  8.7 2.5 %collective-permute-done.1 = f32[128,128]{1,0:T(8,128)S(1)} collective-permute-done((f32[128,128]{1,0:T(8,128)S(1)}, f32[128,128]{1,0:T(8,128)S(1)}, u32[]{:S(2)}, u32[]{:S(2)}) %collective-permute-start.1) | collective-permute-done | bytes 65568 | tf_op jit(solution)/shard_map/ppermute | solution.py:15
  11.2 0.1 collective-permute-done
  11.3 0.0 copy-start
  11.3 0.0 copy-start.1
  11.3 0.1 collective-permute-start.3
  11.4 1.5 %collective-permute-done.3.other_ref = f32[4,128,128]{2,1,0:T(8,128)S(1)} collective-permute-done((f32[4,128,128]{2,1,0:T(8,128)S(1)}, f32[4,128,128]{2,1,0:T(8,128)S(1)}, u32[]{:S(2)}, u32[]{:S(2)}) %collective-permute-start.3) | collective-permute-done | bytes 262176 | tf_op jit(solution)/shard_map/ppermute | solution.py:15
  12.9 0.0 copy-done
  12.9 0.0 copy-done.1
  12.9 2.2 %shard_map.92 = f32[6,2,8,128]{3,2,1,0:T(8,128)} custom-call(f32[4,128,128]{2,1,0:T(8,128)S(1)} %pad_maximum_fusion.own_ref, f32[4,128,128]{2,1,0:T(8,128)S(1)} %collective-permute-done.3.other_ref, s32[1,32]{1,0:T(1,128)S(1)} %bitcast.6, f32[6,32]{1,0:T(8,128)S(1)} %copy-done), custom_call_target="tpu_custom_call" | custom-call | tf_op jit(solution)/shard_map/pallas_call | solution.py:286
  (1 shorter events, 0.0 us)
Async XLA Ops:
  0.9 7.9 %collective-permute-start.2 = (f32[128,128]{1,0:T(8,128)S(1)}, f32[128,128]{1,0:T(8,128)S(1)}, u32[]{:S(2)}, u32[]{:S(2)}) collective-permute-start(f32[128,128]{1,0:T(8,128)S(1)} %shard_map.91), channel_id=1, source_target_pairs={{0,8},{4,12},{8,0},{12,4},{1,9},{5,13},{9,1},{13,5},{2,10},{6,14},... | collective-permute-start | bytes 196616 | tf_op jit(solution)/shard_map/ppermute | solution.py:15
  5.0 6.2 %collective-permute-start.1 = (f32[128,128]{1,0:T(8,128)S(1)}, f32[128,128]{1,0:T(8,128)S(1)}, u32[]{:S(2)}, u32[]{:S(2)}) collective-permute-start(f32[128,128]{1,0:T(8,128)S(1)} %shard_map.91), channel_id=1, source_target_pairs={{0,12},{4,8},{8,4},{12,0},{1,13},{5,9},{9,5},{13,1},{2,14},{6,10},... | collective-permute-start | bytes 196616 | tf_op jit(solution)/shard_map/ppermute | solution.py:15
  6.3 5.0 %collective-permute-start = (f32[128,128]{1,0:T(8,128)S(1)}, f32[128,128]{1,0:T(8,128)S(1)}, u32[]{:S(2)}, u32[]{:S(2)}) collective-permute-start(f32[128,128]{1,0:T(8,128)S(1)} %shard_map.91), channel_id=1, source_target_pairs={{0,4},{4,0},{8,12},{12,8},{1,5},{5,1},{9,13},{13,9},{2,6},{6,2},{1... | collective-permute-start | bytes 196616 | tf_op jit(solution)/shard_map/ppermute | solution.py:15
  11.3 1.6 %copy-start = (f32[6,32]{1,0:T(8,128)S(1)}, f32[6,32]{1,0:T(8,128)}, u32[]{:S(2)}) copy-start(f32[6,32]{1,0:T(8,128)} %prior_ref.1) | copy-start | bytes 2308
  11.3 1.6 %copy-start.1 = (s32[32]{0:T(128)S(1)}, s32[32]{0:T(128)}, u32[]{:S(2)}) copy-start(s32[32]{0:T(128)} %param.16) | copy-start | bytes 388
  11.3 1.6 %collective-permute-start.3 = (f32[4,128,128]{2,1,0:T(8,128)S(1)}, f32[4,128,128]{2,1,0:T(8,128)S(1)}, u32[]{:S(2)}, u32[]{:S(2)}) collective-permute-start(f32[4,128,128]{2,1,0:T(8,128)S(1)} %pad_maximum_fusion.own_ref), channel_id=1, source_target_pairs={{0,2},{2,0},{1,3},{3,1},{4,6},{6,4},{5,7},{7,5},{8,10},{10,8},{9,1... | collective-permute-start | bytes 786440 | tf_op jit(solution)/shard_map/ppermute | solution.py:15

commit v3 on v2

--- a/solution.py
+++ b/solution.py
@@ -16,7 +16,7 @@
 
 
 def slot_of(k, blocks):
-    return jnp.where(k > 1, blocks + 1 - k, k)
+    return jnp.where(k > 1, k - 1, k * (blocks - 1))
 
 
 def transport_kernel(tracers, blocks, regions, own_ref, other_ref, owner_ref, prior_ref, out_ref, flat_ref):
@@ -30,23 +30,22 @@
     first_row, last_row = row == 0, row == SUB - 1
     first_lane, last_lane = lane == 0, lane == LANES - 1
     base = tracers * 2 * SUB
+    stride = base + 3 * SUB
 
     def tile(h, b, at):
-        return bands[h][place[b], at : at + SUB, :]
+        return bands[h][pl.ds(pl.multiple_of(place[b] * stride, SUB) + at, SUB), :]
 
     def full(h, at):
-        return jnp.broadcast_to(bands[h][0, at : at + 1, :], (SUB, LANES))
+        return jnp.broadcast_to(bands[h][at : at + 1, :], (SUB, LANES))
 
     foot = [[tile(h, b, base) for h in range(2)] for b in range(blocks)]
     region = [[tile(h, b, base + SUB).astype(i32) for h in range(2)] for b in range(blocks)]
-    half = [[0.5 * tile(h, b, base + 2 * SUB) for h in range(2)] for b in range(blocks)]
-    at = base + 3 * SUB
+    half = [[tile(h, b, base + 2 * SUB) for h in range(2)] for b in range(blocks)]
+    at = blocks * stride
     shift = [[full(h, at + l).astype(i32) for h in range(2)] for l in range(2)]
-    frac = [[full(h, at + 2 + l) for h in range(2)] for l in range(2)]
-    face = [[full(h, at + 4 + l) for h in range(2)] for l in range(2)]
-    w_left = [[a * (a + 1.0) * 0.5 for a in x] for x in frac]
-    w_centre = [[1.0 - a * a for a in x] for x in frac]
-    w_right = [[a * (a - 1.0) * 0.5 for a in x] for x in frac]
+    face, w_left, w_centre, w_right = (
+        [[full(h, at + 2 * n + l) for h in range(2)] for l in range(2)] for n in range(1, 5)
+    )
 
     def north(v):
         r = [pltpu.roll(x, LANES - 1, 1) for x in v]
@@ -63,13 +62,10 @@
         n, s = north(v), south(v)
         return [face_mid[l][h] * v[h] + face[l][h] * n[h] + face_prev[l][h] * s[h] for h in only]
 
-    def mod(e):
-        return jnp.where(e >= blocks, e - blocks, e)
-
     steps = range((blocks - 1).bit_length())
 
     def bits(e):
-        return [(e >> k) & 1 == 1 for k in steps]
+        return [e & (1 << k) != 0 for k in steps]
 
     def plan(amount, ahead):
         whole, within = amount >> 3, amount & 7
@@ -79,7 +75,7 @@
         else:
             crossed = (row + within >= SUB).astype(i32)
             index = (row - within) & 7
-        return bits(mod(mod(whole + crossed))), index
+        return bits(whole + crossed), index
 
     def pick(v, plan, sign, wanted):
         masks, index = plan
@@ -94,10 +90,8 @@
         return [jnp.take_along_axis(current[b], index, axis=0, mode="promise_in_bounds") for b in wanted]
 
     def beside(v):
-        up = [pltpu.roll(x, SUB - 1, 0) for x in v]
-        down = [pltpu.roll(x, 1, 0) for x in v]
-        after = [jnp.where(last_row, up[(b + 1) % blocks], up[b]) for b in range(blocks)]
-        before = [jnp.where(first_row, down[(b - 1) % blocks], down[b]) for b in range(blocks)]
+        after = [pltpu.roll(jnp.where(first_row, v[(b + 1) % blocks], v[b]), SUB - 1, 0) for b in range(blocks)]
+        before = [pltpu.roll(jnp.where(last_row, v[(b - 1) % blocks], v[b]), 1, 0) for b in range(blocks)]
         return before, after
 
     every = range(blocks)
@@ -136,16 +130,17 @@
     bf16 = jnp.bfloat16
     lines = tracers * SUB
     total = jnp.zeros((3 * lines, SUB * regions), f32)
-    number = lax.broadcasted_iota(i32, (1, regions, 2 * LANES), 1)
+    number = lax.broadcasted_iota(i32, (regions, 2 * LANES), 0).astype(bf16)[None]
     for b in every:
         x = flat_ref[b]
         hi = x.astype(bf16)
         rest = x - hi.astype(f32)
         mid = rest.astype(bf16)
         low = (rest - mid.astype(f32)).astype(bf16)
-        ids = jnp.concatenate(region[b], axis=1)
-        same = ids[:, None, :] == number
-        table = jnp.where(same, 1.0, 0.0).astype(bf16).reshape(SUB * regions, 2 * LANES)
+        ids = jnp.concatenate(region[b], axis=1).astype(f32)
+        ids = jnp.broadcast_to(ids[:, None, :], (SUB, regions, 2 * LANES)).astype(bf16)
+        one, zero = jnp.ones((), bf16), jnp.zeros((), bf16)
+        table = jnp.where(ids == number, one, zero).reshape(SUB * regions, 2 * LANES)
         total = total + lax.dot_general(
             jnp.concatenate([hi, mid, low], axis=0),
             table,
@@ -220,7 +215,7 @@
         out_ref[t, 1] = tile(0, 0, (2 * t + 1) * SUB) * (moved[1] - d)
 
 
-def pack_kernel(tracers, sign_ref, shift_ref, frac_ref, face_ref, convect_ref, foot_ref, region_ref, out_ref, *scratch):
+def pack_kernel(tracers, sign_ref, shift_ref, frac_ref, face_ref, convect_ref, foot_ref, region_ref, out_ref, rows_ref, *scratch):
     f32, i32 = jnp.float32, jnp.int32
     sources = (sign_ref, foot_ref, region_ref, convect_ref, shift_ref, frac_ref, face_ref)
     held, arrived = scratch[:-1], scratch[-1]
@@ -234,18 +229,22 @@
     base = tracers * 2 * SUB
     for n, slot in ((1, foot), (2, region), (3, convect)):
         copies[n].wait()
-        out_ref[base + (n - 1) * SUB : base + n * SUB, :] = slot[...].astype(f32)
+        value = slot[...].astype(f32)
+        out_ref[base + (n - 1) * SUB : base + n * SUB, :] = 0.5 * value if n == 3 else value
     for n in (4, 5, 6):
         copies[n].wait()
     ends = lax.axis_index("lat") == lax.axis_size("lat") - 1
     lane = lax.broadcasted_iota(i32, (2, LANES), 1)
     closed = jnp.where(ends, LANES - 1, LANES)
-    out_ref[base + 3 * SUB : base + 4 * SUB, :] = jnp.concatenate(
+    a = frac[...]
+    rows_ref[...] = jnp.concatenate(
         [
             shift[...].astype(f32),
-            frac[...],
             jnp.where(lane == closed, 0.0, face[...]),
-            jnp.zeros((2, LANES), f32),
+            a * (a + 1.0) * 0.5,
+            1.0 - a * a,
+            a * (a - 1.0) * 0.5,
+            jnp.zeros((6, LANES), f32),
         ],
         axis=0,
     )
@@ -273,15 +272,15 @@
     f32 = jnp.float32
     anywhere = pl.BlockSpec(memory_space=pl.ANY)
     fields = (probe_signs, footprint, region_id, convect_frac, shift_cells, courant_frac, merid_coef)
-    block = pl.pallas_call(
+    block, params = pl.pallas_call(
         functools.partial(pack_kernel, tracers),
-        out_shape=pltpu.VMEM((tracers * levels * width + 4 * SUB, rows), f32),
+        out_shape=(pltpu.VMEM((tracers * levels * width + 3 * SUB, rows), f32), pltpu.VMEM((2 * SUB, rows), f32)),
         in_specs=[anywhere] * 7,
-        out_specs=pl.BlockSpec(memory_space=pltpu.VMEM),
+        out_specs=[pl.BlockSpec(memory_space=pltpu.VMEM)] * 2,
         scratch_shapes=[pltpu.VMEM(x.shape, x.dtype) for x in fields] + [pltpu.SemaphoreType.DMA((7,))],
     )(probe_signs, shift_cells, courant_frac, merid_coef, convect_frac, footprint, region_id)
-    order = sorted(range(1, blocks), key=lambda k: (k > 1, -k))
-    own = jnp.stack([block] + [swapped(block, "lon", k) for k in order])
+    order = [*range(2, blocks), 1]
+    own = jnp.concatenate([block] + [swapped(block, "lon", k) for k in order] + [params])
     other = swapped(own, "lat", 1)
     return pl.pallas_call(
         functools.partial(transport_kernel, tracers, blocks, regions),

time: 15.3 us -> 15.1 us (0.987)
  transfers between devices with their start and end apart: 4 -> 4, of which waited for: 4 -> 3; matrix products, arithmetic and copies ran while one was open for 0% -> 0% of each run, Pallas kernels for 0% -> 0%
where the time goes in v3:
time: 15.1 us; the launch traced here: 14.9 us
  waiting for transfers between devices  6.14 us (41%)
  starting transfers between devices  5.75 us (38%)
  Pallas kernels  2.92 us (19%)
    ppermute x4, waiting for transfers between devices, swapped(): return lax.ppermute(block, axis, [(i, i ^ k) for i in range(size)])  6.14 us
    ppermute x4, starting transfers between devices, swapped(): return lax.ppermute(block, axis, [(i, i ^ k) for i in range(size)])  5.75 us
    pallas_call x1, Pallas kernels, on_device(): pl.pallas_call(functools.partial(transport_kernel, tracers, blocks, regio...  2.06 us
    pallas_call x1, Pallas kernels, on_device(): pl.pallas_call(functools.partial(pack_kernel, tracers), out_shape=(pltpu....  0.87 us
  transfers between devices with their start and end apart: 4, of which 3 were waited for; matrix products, arithmetic and copies ran while one was open for 0% of the time, Pallas kernels for 0%

profile of v3, /device:TPU:0, one launch (start us, length us, event | category | flops | bytes accessed | tf_op | source)
XLA Modules:
  0.0 14.9 jit_solution(1625705313928749257)
XLA Ops:
  0.0 0.9 %shard_map.91 = (f32[120,128]{1,0:T(8,128)S(1)}, f32[16,128]{1,0:T(8,128)S(1)}) custom-call(s32[6,2,8,128]{3,2,1,0:T(8,128)} %sign_ref.1, s32[2,128]{1,0:T(2,128)} %shift_ref.1, f32[2,128]{1,0:T(2,128)} %frac_ref.1, f32[2,128]{1,0:T(2,128)} %face_ref.1, f32[8,128]{1,0:T(8,128)} %convect_ref.1, f32[8,128]{1,0:T(8,128)} %foot_ref.1, s32[8,128]{1,0:T(8,128)} %region_ref.1), custom_call_target="tpu_custom_call" | custom-call | tf_op jit(solution)/shard_map/pallas_call | solution.py:275
  0.9 4.1 %collective-permute-start = (f32[120,128]{1,0:T(8,128)S(1)}, f32[120,128]{1,0:T(8,128)S(1)}, u32[]{:S(2)}, u32[]{:S(2)}) collective-permute-start(f32[120,128]{1,0:T(8,128)S(1)} %get-tuple-element.7), channel_id=1, source_target_pairs={{0,8},{4,12},{8,0},{12,4},{1,9},{5,13},{9,1},{13,5},{2,10},{6,14},... | collective-permute-start | bytes 184328 | tf_op jit(solution)/shard_map/ppermute | solution.py:15
  5.0 1.3 %collective-permute-start.1 = (f32[120,128]{1,0:T(8,128)S(1)}, f32[120,128]{1,0:T(8,128)S(1)}, u32[]{:S(2)}, u32[]{:S(2)}) collective-permute-start(f32[120,128]{1,0:T(8,128)S(1)} %get-tuple-element.7), channel_id=1, source_target_pairs={{0,12},{4,8},{8,4},{12,0},{1,13},{5,9},{9,5},{13,1},{2,14},{6,10},... | collective-permute-start | bytes 184328 | tf_op jit(solution)/shard_map/ppermute | solution.py:15
  6.3 0.2 %collective-permute-start.2 = (f32[120,128]{1,0:T(8,128)S(1)}, f32[120,128]{1,0:T(8,128)S(1)}, u32[]{:S(2)}, u32[]{:S(2)}) collective-permute-start(f32[120,128]{1,0:T(8,128)S(1)} %get-tuple-element.7), channel_id=1, source_target_pairs={{0,4},{4,0},{8,12},{12,8},{1,5},{5,1},{9,13},{13,9},{2,6},{6,2},{1... | collective-permute-start | bytes 184328 | tf_op jit(solution)/shard_map/ppermute | solution.py:15
  6.6 1.3 %collective-permute-done = f32[120,128]{1,0:T(8,128)S(1)} collective-permute-done((f32[120,128]{1,0:T(8,128)S(1)}, f32[120,128]{1,0:T(8,128)S(1)}, u32[]{:S(2)}, u32[]{:S(2)}) %collective-permute-start) | collective-permute-done | bytes 61472 | tf_op jit(solution)/shard_map/ppermute | solution.py:15
  7.8 3.3 %collective-permute-done.1 = f32[120,128]{1,0:T(8,128)S(1)} collective-permute-done((f32[120,128]{1,0:T(8,128)S(1)}, f32[120,128]{1,0:T(8,128)S(1)}, u32[]{:S(2)}, u32[]{:S(2)}) %collective-permute-start.1) | collective-permute-done | bytes 61472 | tf_op jit(solution)/shard_map/ppermute | solution.py:15
  11.2 0.0 collective-permute-done.2
  11.2 0.0 copy-start
  11.2 0.0 copy-start.1
  11.2 0.1 collective-permute-start.3
  11.3 1.5 %collective-permute-done.3.other_ref = f32[496,128]{1,0:T(8,128)S(1)} collective-permute-done((f32[496,128]{1,0:T(8,128)S(1)}, f32[496,128]{1,0:T(8,128)S(1)}, u32[]{:S(2)}, u32[]{:S(2)}) %collective-permute-start.3) | collective-permute-done | bytes 253984 | tf_op jit(solution)/shard_map/ppermute | solution.py:15
  12.8 0.0 copy-done
  12.8 0.0 copy-done.1
  12.8 2.1 %shard_map.92 = f32[6,2,8,128]{3,2,1,0:T(8,128)} custom-call(f32[496,128]{1,0:T(8,128)S(1)} %constant_dynamic-update-slice_fusion.own_ref, f32[496,128]{1,0:T(8,128)S(1)} %collective-permute-done.3.other_ref, s32[1,32]{1,0:T(1,128)S(1)} %bitcast.1, f32[6,32]{1,0:T(8,128)S(1)} %copy-done), custom_call_target="tpu_custom_call" | custom-call | tf_op jit(solution)/shard_map/pallas_call | solution.py:285
  (5 shorter events, 0.0 us)
Async XLA Ops:
  0.9 7.0 %collective-permute-start = (f32[120,128]{1,0:T(8,128)S(1)}, f32[120,128]{1,0:T(8,128)S(1)}, u32[]{:S(2)}, u32[]{:S(2)}) collective-permute-start(f32[120,128]{1,0:T(8,128)S(1)} %get-tuple-element.7), channel_id=1, source_target_pairs={{0,8},{4,12},{8,0},{12,4},{1,9},{5,13},{9,1},{13,5},{2,10},{6,14},... | collective-permute-start | bytes 184328 | tf_op jit(solution)/shard_map/ppermute | solution.py:15
  5.0 6.2 %collective-permute-start.1 = (f32[120,128]{1,0:T(8,128)S(1)}, f32[120,128]{1,0:T(8,128)S(1)}, u32[]{:S(2)}, u32[]{:S(2)}) collective-permute-start(f32[120,128]{1,0:T(8,128)S(1)} %get-tuple-element.7), channel_id=1, source_target_pairs={{0,12},{4,8},{8,4},{12,0},{1,13},{5,9},{9,5},{13,1},{2,14},{6,10},... | collective-permute-start | bytes 184328 | tf_op jit(solution)/shard_map/ppermute | solution.py:15
  6.3 4.9 %collective-permute-start.2 = (f32[120,128]{1,0:T(8,128)S(1)}, f32[120,128]{1,0:T(8,128)S(1)}, u32[]{:S(2)}, u32[]{:S(2)}) collective-permute-start(f32[120,128]{1,0:T(8,128)S(1)} %get-tuple-element.7), channel_id=1, source_target_pairs={{0,4},{4,0},{8,12},{12,8},{1,5},{5,1},{9,13},{13,9},{2,6},{6,2},{1... | collective-permute-start | bytes 184328 | tf_op jit(solution)/shard_map/ppermute | solution.py:15
  11.2 1.6 %copy-start = (f32[6,32]{1,0:T(8,128)S(1)}, f32[6,32]{1,0:T(8,128)}, u32[]{:S(2)}) copy-start(f32[6,32]{1,0:T(8,128)} %prior_ref.1) | copy-start | bytes 2308
  11.2 1.6 %copy-start.1 = (s32[32]{0:T(128)S(1)}, s32[32]{0:T(128)}, u32[]{:S(2)}) copy-start(s32[32]{0:T(128)} %param.16) | copy-start | bytes 388
  11.2 1.6 %collective-permute-start.3 = (f32[496,128]{1,0:T(8,128)S(1)}, f32[496,128]{1,0:T(8,128)S(1)}, u32[]{:S(2)}, u32[]{:S(2)}) collective-permute-start(f32[496,128]{1,0:T(8,128)S(1)} %constant_dynamic-update-slice_fusion.own_ref), channel_id=1, source_target_pairs={{0,2},{2,0},{1,3},{3,1},{4,6},{6,4},{5,7},{7,5},{8,10},{10,8},{9,1... | collective-permute-start | bytes 761864 | tf_op jit(solution)/shard_map/ppermute | solution.py:15

commit v4 on v3

--- a/solution.py
+++ b/solution.py
@@ -15,14 +15,20 @@
     return lax.ppermute(block, axis, [(i, i ^ k) for i in range(size)])
 
 
-def slot_of(k, blocks):
-    return jnp.where(k > 1, k - 1, k * (blocks - 1))
+def ring(i):
+    return i ^ (i >> 1)
+
+
+def turned(block, k):
+    size = lax.axis_size("lon")
+    spot = {ring(i): i for i in range(size)}
+    return lax.ppermute(block, "lon", [(i, spot[(ring(i) + k) % size]) for i in range(size)])
 
 
 def transport_kernel(tracers, blocks, regions, own_ref, other_ref, owner_ref, prior_ref, out_ref, flat_ref):
     f32, i32 = jnp.float32, jnp.int32
     me = lax.axis_index("lon")
-    place = [slot_of(me ^ ((me + b) % blocks), blocks) if b else 0 for b in range(blocks)]
+    place = [(ring(me) - ring((me + b) % blocks)) % blocks if b else 0 for b in range(blocks)]
     bands = (own_ref, other_ref)
     cycle = blocks * SUB
     row = lax.broadcasted_iota(i32, (SUB, LANES), 0)
@@ -279,8 +285,7 @@
         out_specs=[pl.BlockSpec(memory_space=pltpu.VMEM)] * 2,
         scratch_shapes=[pltpu.VMEM(x.shape, x.dtype) for x in fields] + [pltpu.SemaphoreType.DMA((7,))],
     )(probe_signs, shift_cells, courant_frac, merid_coef, convect_frac, footprint, region_id)
-    order = [*range(2, blocks), 1]
-    own = jnp.concatenate([block] + [swapped(block, "lon", k) for k in order] + [params])
+    own = jnp.concatenate([block] + [turned(block, k) for k in range(1, blocks)] + [params])
     other = swapped(own, "lat", 1)
     return pl.pallas_call(
         functools.partial(transport_kernel, tracers, blocks, regions),

time: 15.1 us -> 14.9 us (0.987)
  waiting for transfers between devices: 6.14 us -> 4.52 us
  starting transfers between devices: 5.75 us -> 7.2 us
    ppermute x0 -> x3, starting transfers between devices: none -> 7.13 us  [turned(): lax.ppermute(block, 'lon', [(i, spot[(ring(i) + k) % size]) for i in rang...]
    ppermute x4 -> x1, starting transfers between devices: 5.75 us -> 0.07 us  [swapped(): return lax.ppermute(block, axis, [(i, i ^ k) for i in range(size)])]
    ppermute x4 -> x1, waiting for transfers between devices: 6.14 us -> 1.51 us  [swapped(): return lax.ppermute(block, axis, [(i, i ^ k) for i in range(size)])]
    ppermute x0 -> x3, waiting for transfers between devices: none -> 3.01 us  [turned(): lax.ppermute(block, 'lon', [(i, spot[(ring(i) + k) % size]) for i in rang...]
where the time goes in v4:
time: 14.9 us; the launch traced here: 14.7 us
  starting transfers between devices  7.2 us (48%)
  waiting for transfers between devices  4.52 us (30%)
  Pallas kernels  2.93 us (20%)
    ppermute x3, starting transfers between devices, turned(): lax.ppermute(block, 'lon', [(i, spot[(ring(i) + k) % size]) for i in rang...  7.13 us
    ppermute x3, waiting for transfers between devices, turned(): lax.ppermute(block, 'lon', [(i, spot[(ring(i) + k) % size]) for i in rang...  3.01 us
    pallas_call x1, Pallas kernels, on_device(): pl.pallas_call(functools.partial(transport_kernel, tracers, blocks, regio...  2.07 us
    ppermute x1, waiting for transfers between devices, swapped(): return lax.ppermute(block, axis, [(i, i ^ k) for i in range(size)])  1.51 us
    pallas_call x1, Pallas kernels, on_device(): pl.pallas_call(functools.partial(pack_kernel, tracers), out_shape=(pltpu....  0.87 us
  transfers between devices with their start and end apart: 4, of which 3 were waited for; matrix products, arithmetic and copies ran while one was open for 0% of the time, Pallas kernels for 0%

profile of v4, /device:TPU:0, one launch (start us, length us, event | category | flops | bytes accessed | tf_op | source)
XLA Modules:
  0.0 14.7 jit_solution(11266078697657111506)
XLA Ops:
  0.0 0.9 %shard_map.91 = (f32[120,128]{1,0:T(8,128)S(1)}, f32[16,128]{1,0:T(8,128)S(1)}) custom-call(s32[6,2,8,128]{3,2,1,0:T(8,128)} %sign_ref.1, s32[2,128]{1,0:T(2,128)} %shift_ref.1, f32[2,128]{1,0:T(2,128)} %frac_ref.1, f32[2,128]{1,0:T(2,128)} %face_ref.1, f32[8,128]{1,0:T(8,128)} %convect_ref.1, f32[8,128]{1,0:T(8,128)} %foot_ref.1, s32[8,128]{1,0:T(8,128)} %region_ref.1), custom_call_target="tpu_custom_call" | custom-call | tf_op jit(solution)/shard_map/pallas_call | solution.py:281
  0.9 3.1 %collective-permute-start = (f32[120,128]{1,0:T(8,128)S(1)}, f32[120,128]{1,0:T(8,128)S(1)}, u32[]{:S(2)}, u32[]{:S(2)}) collective-permute-start(f32[120,128]{1,0:T(8,128)S(1)} %get-tuple-element.7), channel_id=1, source_target_pairs={{0,4},{4,12},{8,0},{12,8},{1,5},{5,13},{9,1},{13,9},{2,6},{6,14},{... | collective-permute-start | bytes 184328 | tf_op jit(solution)/shard_map/ppermute | solution.py:25
  4.0 2.5 %collective-permute-start.1 = (f32[120,128]{1,0:T(8,128)S(1)}, f32[120,128]{1,0:T(8,128)S(1)}, u32[]{:S(2)}, u32[]{:S(2)}) collective-permute-start(f32[120,128]{1,0:T(8,128)S(1)} %get-tuple-element.7), channel_id=1, source_target_pairs={{0,12},{4,8},{8,4},{12,0},{1,13},{5,9},{9,5},{13,1},{2,14},{6,10},... | collective-permute-start | bytes 184328 | tf_op jit(solution)/shard_map/ppermute | solution.py:25
  6.4 1.6 %collective-permute-start.2 = (f32[120,128]{1,0:T(8,128)S(1)}, f32[120,128]{1,0:T(8,128)S(1)}, u32[]{:S(2)}, u32[]{:S(2)}) collective-permute-start(f32[120,128]{1,0:T(8,128)S(1)} %get-tuple-element.7), channel_id=1, source_target_pairs={{0,8},{4,0},{8,12},{12,4},{1,9},{5,1},{9,13},{13,5},{2,10},{6,2},{... | collective-permute-start | bytes 184328 | tf_op jit(solution)/shard_map/ppermute | solution.py:25
  8.0 0.0 collective-permute-done
  8.0 2.7 %collective-permute-done.1 = f32[120,128]{1,0:T(8,128)S(1)} collective-permute-done((f32[120,128]{1,0:T(8,128)S(1)}, f32[120,128]{1,0:T(8,128)S(1)}, u32[]{:S(2)}, u32[]{:S(2)}) %collective-permute-start.1) | collective-permute-done | bytes 61472 | tf_op jit(solution)/shard_map/ppermute | solution.py:25
  10.7 0.3 %collective-permute-done.2 = f32[120,128]{1,0:T(8,128)S(1)} collective-permute-done((f32[120,128]{1,0:T(8,128)S(1)}, f32[120,128]{1,0:T(8,128)S(1)}, u32[]{:S(2)}, u32[]{:S(2)}) %collective-permute-start.2) | collective-permute-done | bytes 61472 | tf_op jit(solution)/shard_map/ppermute | solution.py:25
  11.1 0.0 copy-start
  11.1 0.0 copy-start.1
  11.1 0.1 collective-permute-start.3
  11.2 1.5 %collective-permute-done.3.other_ref = f32[496,128]{1,0:T(8,128)S(1)} collective-permute-done((f32[496,128]{1,0:T(8,128)S(1)}, f32[496,128]{1,0:T(8,128)S(1)}, u32[]{:S(2)}, u32[]{:S(2)}) %collective-permute-start.3) | collective-permute-done | bytes 253984 | tf_op jit(solution)/shard_map/ppermute | solution.py:15
  12.7 0.0 copy-done
  12.7 0.0 copy-done.1
  12.7 2.1 %shard_map.92 = f32[6,2,8,128]{3,2,1,0:T(8,128)} custom-call(f32[496,128]{1,0:T(8,128)S(1)} %constant_dynamic-update-slice_fusion.own_ref, f32[496,128]{1,0:T(8,128)S(1)} %collective-permute-done.3.other_ref, s32[1,32]{1,0:T(1,128)S(1)} %bitcast.1, f32[6,32]{1,0:T(8,128)S(1)} %copy-done), custom_call_target="tpu_custom_call" | custom-call | tf_op jit(solution)/shard_map/pallas_call | solution.py:290
  (5 shorter events, 0.0 us)
Async XLA Ops:
  0.9 7.1 %collective-permute-start = (f32[120,128]{1,0:T(8,128)S(1)}, f32[120,128]{1,0:T(8,128)S(1)}, u32[]{:S(2)}, u32[]{:S(2)}) collective-permute-start(f32[120,128]{1,0:T(8,128)S(1)} %get-tuple-element.7), channel_id=1, source_target_pairs={{0,4},{4,12},{8,0},{12,8},{1,5},{5,13},{9,1},{13,9},{2,6},{6,14},{... | collective-permute-start | bytes 184328 | tf_op jit(solution)/shard_map/ppermute | solution.py:25
  4.0 6.8 %collective-permute-start.1 = (f32[120,128]{1,0:T(8,128)S(1)}, f32[120,128]{1,0:T(8,128)S(1)}, u32[]{:S(2)}, u32[]{:S(2)}) collective-permute-start(f32[120,128]{1,0:T(8,128)S(1)} %get-tuple-element.7), channel_id=1, source_target_pairs={{0,12},{4,8},{8,4},{12,0},{1,13},{5,9},{9,5},{13,1},{2,14},{6,10},... | collective-permute-start | bytes 184328 | tf_op jit(solution)/shard_map/ppermute | solution.py:25
  6.4 4.6 %collective-permute-start.2 = (f32[120,128]{1,0:T(8,128)S(1)}, f32[120,128]{1,0:T(8,128)S(1)}, u32[]{:S(2)}, u32[]{:S(2)}) collective-permute-start(f32[120,128]{1,0:T(8,128)S(1)} %get-tuple-element.7), channel_id=1, source_target_pairs={{0,8},{4,0},{8,12},{12,4},{1,9},{5,1},{9,13},{13,5},{2,10},{6,2},{... | collective-permute-start | bytes 184328 | tf_op jit(solution)/shard_map/ppermute | solution.py:25
  11.1 1.6 %copy-start = (f32[6,32]{1,0:T(8,128)S(1)}, f32[6,32]{1,0:T(8,128)}, u32[]{:S(2)}) copy-start(f32[6,32]{1,0:T(8,128)} %prior_ref.1) | copy-start | bytes 2308
  11.1 1.6 %copy-start.1 = (s32[32]{0:T(128)S(1)}, s32[32]{0:T(128)}, u32[]{:S(2)}) copy-start(s32[32]{0:T(128)} %param.16) | copy-start | bytes 388
  11.1 1.6 %collective-permute-start.3 = (f32[496,128]{1,0:T(8,128)S(1)}, f32[496,128]{1,0:T(8,128)S(1)}, u32[]{:S(2)}, u32[]{:S(2)}) collective-permute-start(f32[496,128]{1,0:T(8,128)S(1)} %constant_dynamic-update-slice_fusion.own_ref), channel_id=1, source_target_pairs={{0,2},{2,0},{1,3},{3,1},{4,6},{6,4},{5,7},{7,5},{8,10},{10,8},{9,1... | collective-permute-start | bytes 761864 | tf_op jit(solution)/shard_map/ppermute | solution.py:15

commit v5 on v4

--- a/solution.py
+++ b/solution.py
@@ -135,25 +135,24 @@
 
     bf16 = jnp.bfloat16
     lines = tracers * SUB
-    total = jnp.zeros((3 * lines, SUB * regions), f32)
+    total = jnp.zeros((2 * lines, SUB * regions), f32)
     number = lax.broadcasted_iota(i32, (regions, 2 * LANES), 0).astype(bf16)[None]
     for b in every:
         x = flat_ref[b]
         hi = x.astype(bf16)
         rest = x - hi.astype(f32)
         mid = rest.astype(bf16)
-        low = (rest - mid.astype(f32)).astype(bf16)
         ids = jnp.concatenate(region[b], axis=1).astype(f32)
         ids = jnp.broadcast_to(ids[:, None, :], (SUB, regions, 2 * LANES)).astype(bf16)
         one, zero = jnp.ones((), bf16), jnp.zeros((), bf16)
         table = jnp.where(ids == number, one, zero).reshape(SUB * regions, 2 * LANES)
         total = total + lax.dot_general(
-            jnp.concatenate([hi, mid, low], axis=0),
+            jnp.concatenate([hi, mid], axis=0),
             table,
             (((1,), (1,)), ((), ())),
             preferred_element_type=f32,
         )
-    sums = total[:lines] + total[lines : 2 * lines] + total[2 * lines :]
+    sums = total[:lines] + total[lines : 2 * lines]
     width = SUB * regions
     column = lax.broadcasted_iota(i32, (SUB, width), 1)
     keep = column // regions == lax.broadcasted_iota(i32, (SUB, width), 0)

time: 14.9 us -> 14.9 us (level)
  no operation moved by 1% of the time
where the time goes in v5:
time: 14.9 us; the launch traced here: 14.7 us
  starting transfers between devices  7.2 us (48%)
  waiting for transfers between devices  4.52 us (30%)
  Pallas kernels  2.9 us (19%)
    ppermute x3, starting transfers between devices, turned(): lax.ppermute(block, 'lon', [(i, spot[(ring(i) + k) % size]) for i in rang...  7.13 us
    ppermute x3, waiting for transfers between devices, turned(): lax.ppermute(block, 'lon', [(i, spot[(ring(i) + k) % size]) for i in rang...  3.01 us
    pallas_call x1, Pallas kernels, on_device(): pl.pallas_call(functools.partial(transport_kernel, tracers, blocks, regio...  2.03 us
    ppermute x1, waiting for transfers between devices, swapped(): return lax.ppermute(block, axis, [(i, i ^ k) for i in range(size)])  1.51 us
    pallas_call x1, Pallas kernels, on_device(): pl.pallas_call(functools.partial(pack_kernel, tracers), out_shape=(pltpu....  0.87 us
  transfers between devices with their start and end apart: 4, of which 3 were waited for; matrix products, arithmetic and copies ran while one was open for 0% of the time, Pallas kernels for 0%

profile of v5, /device:TPU:0, one launch (start us, length us, event | category | flops | bytes accessed | tf_op | source)
XLA Modules:
  0.0 14.7 jit_solution(13171680257048625714)
XLA Ops:
  0.0 0.9 %shard_map.91 = (f32[120,128]{1,0:T(8,128)S(1)}, f32[16,128]{1,0:T(8,128)S(1)}) custom-call(s32[6,2,8,128]{3,2,1,0:T(8,128)} %sign_ref.1, s32[2,128]{1,0:T(2,128)} %shift_ref.1, f32[2,128]{1,0:T(2,128)} %frac_ref.1, f32[2,128]{1,0:T(2,128)} %face_ref.1, f32[8,128]{1,0:T(8,128)} %convect_ref.1, f32[8,128]{1,0:T(8,128)} %foot_ref.1, s32[8,128]{1,0:T(8,128)} %region_ref.1), custom_call_target="tpu_custom_call" | custom-call | tf_op jit(solution)/shard_map/pallas_call | solution.py:280
  0.9 3.1 %collective-permute-start = (f32[120,128]{1,0:T(8,128)S(1)}, f32[120,128]{1,0:T(8,128)S(1)}, u32[]{:S(2)}, u32[]{:S(2)}) collective-permute-start(f32[120,128]{1,0:T(8,128)S(1)} %get-tuple-element.7), channel_id=1, source_target_pairs={{0,4},{4,12},{8,0},{12,8},{1,5},{5,13},{9,1},{13,9},{2,6},{6,14},{... | collective-permute-start | bytes 184328 | tf_op jit(solution)/shard_map/ppermute | solution.py:25
  4.0 2.5 %collective-permute-start.1 = (f32[120,128]{1,0:T(8,128)S(1)}, f32[120,128]{1,0:T(8,128)S(1)}, u32[]{:S(2)}, u32[]{:S(2)}) collective-permute-start(f32[120,128]{1,0:T(8,128)S(1)} %get-tuple-element.7), channel_id=1, source_target_pairs={{0,12},{4,8},{8,4},{12,0},{1,13},{5,9},{9,5},{13,1},{2,14},{6,10},... | collective-permute-start | bytes 184328 | tf_op jit(solution)/shard_map/ppermute | solution.py:25
  6.4 1.6 %collective-permute-start.2 = (f32[120,128]{1,0:T(8,128)S(1)}, f32[120,128]{1,0:T(8,128)S(1)}, u32[]{:S(2)}, u32[]{:S(2)}) collective-permute-start(f32[120,128]{1,0:T(8,128)S(1)} %get-tuple-element.7), channel_id=1, source_target_pairs={{0,8},{4,0},{8,12},{12,4},{1,9},{5,1},{9,13},{13,5},{2,10},{6,2},{... | collective-permute-start | bytes 184328 | tf_op jit(solution)/shard_map/ppermute | solution.py:25
  8.0 0.0 collective-permute-done
  8.0 2.7 %collective-permute-done.1 = f32[120,128]{1,0:T(8,128)S(1)} collective-permute-done((f32[120,128]{1,0:T(8,128)S(1)}, f32[120,128]{1,0:T(8,128)S(1)}, u32[]{:S(2)}, u32[]{:S(2)}) %collective-permute-start.1) | collective-permute-done | bytes 61472 | tf_op jit(solution)/shard_map/ppermute | solution.py:25
  10.7 0.3 %collective-permute-done.2 = f32[120,128]{1,0:T(8,128)S(1)} collective-permute-done((f32[120,128]{1,0:T(8,128)S(1)}, f32[120,128]{1,0:T(8,128)S(1)}, u32[]{:S(2)}, u32[]{:S(2)}) %collective-permute-start.2) | collective-permute-done | bytes 61472 | tf_op jit(solution)/shard_map/ppermute | solution.py:25
  11.1 0.0 copy-start
  11.1 0.0 copy-start.1
  11.1 0.1 collective-permute-start.3
  11.2 1.5 %collective-permute-done.3.other_ref = f32[496,128]{1,0:T(8,128)S(1)} collective-permute-done((f32[496,128]{1,0:T(8,128)S(1)}, f32[496,128]{1,0:T(8,128)S(1)}, u32[]{:S(2)}, u32[]{:S(2)}) %collective-permute-start.3) | collective-permute-done | bytes 253984 | tf_op jit(solution)/shard_map/ppermute | solution.py:15
  12.7 0.0 copy-done
  12.7 0.0 copy-done.1
  12.7 2.0 %shard_map.92 = f32[6,2,8,128]{3,2,1,0:T(8,128)} custom-call(f32[496,128]{1,0:T(8,128)S(1)} %constant_dynamic-update-slice_fusion.own_ref, f32[496,128]{1,0:T(8,128)S(1)} %collective-permute-done.3.other_ref, s32[1,32]{1,0:T(1,128)S(1)} %bitcast.1, f32[6,32]{1,0:T(8,128)S(1)} %copy-done), custom_call_target="tpu_custom_call" | custom-call | tf_op jit(solution)/shard_map/pallas_call | solution.py:289
  (5 shorter events, 0.0 us)
Async XLA Ops:
  0.9 7.1 %collective-permute-start = (f32[120,128]{1,0:T(8,128)S(1)}, f32[120,128]{1,0:T(8,128)S(1)}, u32[]{:S(2)}, u32[]{:S(2)}) collective-permute-start(f32[120,128]{1,0:T(8,128)S(1)} %get-tuple-element.7), channel_id=1, source_target_pairs={{0,4},{4,12},{8,0},{12,8},{1,5},{5,13},{9,1},{13,9},{2,6},{6,14},{... | collective-permute-start | bytes 184328 | tf_op jit(solution)/shard_map/ppermute | solution.py:25
  4.0 6.8 %collective-permute-start.1 = (f32[120,128]{1,0:T(8,128)S(1)}, f32[120,128]{1,0:T(8,128)S(1)}, u32[]{:S(2)}, u32[]{:S(2)}) collective-permute-start(f32[120,128]{1,0:T(8,128)S(1)} %get-tuple-element.7), channel_id=1, source_target_pairs={{0,12},{4,8},{8,4},{12,0},{1,13},{5,9},{9,5},{13,1},{2,14},{6,10},... | collective-permute-start | bytes 184328 | tf_op jit(solution)/shard_map/ppermute | solution.py:25
  6.4 4.6 %collective-permute-start.2 = (f32[120,128]{1,0:T(8,128)S(1)}, f32[120,128]{1,0:T(8,128)S(1)}, u32[]{:S(2)}, u32[]{:S(2)}) collective-permute-start(f32[120,128]{1,0:T(8,128)S(1)} %get-tuple-element.7), channel_id=1, source_target_pairs={{0,8},{4,0},{8,12},{12,4},{1,9},{5,1},{9,13},{13,5},{2,10},{6,2},{... | collective-permute-start | bytes 184328 | tf_op jit(solution)/shard_map/ppermute | solution.py:25
  11.1 1.6 %copy-start = (f32[6,32]{1,0:T(8,128)S(1)}, f32[6,32]{1,0:T(8,128)}, u32[]{:S(2)}) copy-start(f32[6,32]{1,0:T(8,128)} %prior_ref.1) | copy-start | bytes 2308
  11.1 1.6 %copy-start.1 = (s32[32]{0:T(128)S(1)}, s32[32]{0:T(128)}, u32[]{:S(2)}) copy-start(s32[32]{0:T(128)} %param.16) | copy-start | bytes 388
  11.1 1.6 %collective-permute-start.3 = (f32[496,128]{1,0:T(8,128)S(1)}, f32[496,128]{1,0:T(8,128)S(1)}, u32[]{:S(2)}, u32[]{:S(2)}) collective-permute-start(f32[496,128]{1,0:T(8,128)S(1)} %constant_dynamic-update-slice_fusion.own_ref), channel_id=1, source_target_pairs={{0,2},{2,0},{1,3},{3,1},{4,6},{6,4},{5,7},{7,5},{8,10},{10,8},{9,1... | collective-permute-start | bytes 761864 | tf_op jit(solution)/shard_map/ppermute | solution.py:15

commit v6 on v5

--- a/solution.py
+++ b/solution.py
@@ -25,7 +25,7 @@
     return lax.ppermute(block, "lon", [(i, spot[(ring(i) + k) % size]) for i in range(size)])
 
 
-def transport_kernel(tracers, blocks, regions, own_ref, other_ref, owner_ref, prior_ref, out_ref, flat_ref):
+def transport_kernel(tracers, blocks, regions, own_ref, other_ref, owner_ref, prior_ref, out_ref, flat_ref, scaled_ref):
     f32, i32 = jnp.float32, jnp.int32
     me = lax.axis_index("lon")
     place = [(ring(me) - ring((me + b) % blocks)) % blocks if b else 0 for b in range(blocks)]
@@ -117,6 +117,7 @@
             )
         return [[result[h][b] for h in range(2)] for b in every]
 
+    flat_ref[:, :, tracers * SUB :, :] = jnp.zeros((blocks, 2, (SUB - tracers) * SUB, LANES), f32)
     for t in range(tracers):
         v = [[[tile(h, b, (2 * t + l) * SUB) for h in range(2)] for b in every] for l in range(2)]
         mixed = [[], []]
@@ -131,46 +132,28 @@
         v = zonal_adjoint(mixed, 0)
         for b in every:
             for h in range(2):
-                flat_ref[b, t * SUB : (t + 1) * SUB, h * LANES : (h + 1) * LANES] = foot[b][h] * v[b][h]
+                flat_ref[b, h, t * SUB : (t + 1) * SUB, :] = foot[b][h] * v[b][h]
 
     bf16 = jnp.bfloat16
-    lines = tracers * SUB
-    total = jnp.zeros((2 * lines, SUB * regions), f32)
     number = lax.broadcasted_iota(i32, (regions, 2 * LANES), 0).astype(bf16)[None]
+    one, zero = jnp.ones((), bf16), jnp.zeros((), bf16)
+    total = jnp.zeros((2 * SUB, regions), f32)
     for b in every:
-        x = flat_ref[b]
-        hi = x.astype(bf16)
-        rest = x - hi.astype(f32)
-        mid = rest.astype(bf16)
         ids = jnp.concatenate(region[b], axis=1).astype(f32)
         ids = jnp.broadcast_to(ids[:, None, :], (SUB, regions, 2 * LANES)).astype(bf16)
-        one, zero = jnp.ones((), bf16), jnp.zeros((), bf16)
-        table = jnp.where(ids == number, one, zero).reshape(SUB * regions, 2 * LANES)
+        table = jnp.where(ids == number, one, zero)
+        parts = []
+        for i in range(SUB):
+            x = jnp.concatenate([flat_ref[b, h, pl.ds(i, SUB, stride=SUB), :] for h in range(2)], axis=1)
+            high = x.astype(bf16).astype(f32)
+            parts.append(jnp.concatenate([high, x - high], axis=0).astype(bf16))
         total = total + lax.dot_general(
-            jnp.concatenate([hi, mid], axis=0),
-            table,
+            jnp.concatenate(parts, axis=1),
+            jnp.concatenate([table[i] for i in range(SUB)], axis=1),
             (((1,), (1,)), ((), ())),
             preferred_element_type=f32,
         )
-    sums = total[:lines] + total[lines : 2 * lines]
-    width = SUB * regions
-    column = lax.broadcasted_iota(i32, (SUB, width), 1)
-    keep = column // regions == lax.broadcasted_iota(i32, (SUB, width), 0)
-    sums = jnp.concatenate(
-        [
-            jnp.sum(jnp.where(keep, sums[t * SUB : (t + 1) * SUB], 0.0), axis=0, keepdims=True)
-            for t in range(tracers)
-        ],
-        axis=0,
-    )
-    while width > max(regions, LANES):
-        width //= 2
-        sums = sums[:, :width] + sums[:, width:]
-    period = width
-    while period > regions:
-        period //= 2
-        sums = sums + pltpu.roll(sums, period, 1)
-    spot = lax.broadcasted_iota(i32, (width, regions), 0) % regions
+    spot = lax.broadcasted_iota(i32, (regions, regions), 0)
     holds = jnp.where(spot == owner_ref[...], 1.0, 0.0)
     prior = lax.dot_general(
         prior_ref[...],
@@ -179,11 +162,12 @@
         precision=lax.Precision.HIGHEST,
         preferred_element_type=f32,
     )
-    scaled = sums * prior
+    scaled_ref[:tracers, :regions] = (total[:SUB] + total[SUB:])[:tracers] * prior
+    width = scaled_ref.shape[1]
 
     keep0 = [[1.0 - x for x in y] for y in half]
     for t in range(tracers):
-        rows = jnp.broadcast_to(scaled[t : t + 1], (SUB, width))
+        rows = jnp.broadcast_to(scaled_ref[t : t + 1, :], (SUB, width))
 
         def spread(ids):
             result = None
@@ -291,7 +275,10 @@
         out_shape=jax.ShapeDtypeStruct(probe_signs.shape, f32),
         in_specs=[pl.BlockSpec(memory_space=pltpu.VMEM)] * 4,
         out_specs=pl.BlockSpec(memory_space=pltpu.VMEM),
-        scratch_shapes=[pltpu.VMEM((blocks, tracers * SUB, 2 * LANES), f32)],
+        scratch_shapes=[
+            pltpu.VMEM((blocks, 2, SUB * SUB, LANES), f32),
+            pltpu.VMEM((tracers, max(regions, LANES)), f32),
+        ],
         compiler_params=pltpu.CompilerParams(vmem_limit_bytes=48 * 1024 * 1024),
     )(own, other, owner_slots.reshape(1, regions), prior_slot)
 

time: 14.9 us -> 14.8 us (level)
  no operation moved by 1% of the time
where the time goes in v6:
time: 14.8 us; the launch traced here: 14.7 us
  starting transfers between devices  7.2 us (49%)
  waiting for transfers between devices  4.52 us (31%)
  Pallas kernels  2.85 us (19%)
    ppermute x3, starting transfers between devices, turned(): lax.ppermute(block, 'lon', [(i, spot[(ring(i) + k) % size]) for i in rang...  7.13 us
    ppermute x3, waiting for transfers between devices, turned(): lax.ppermute(block, 'lon', [(i, spot[(ring(i) + k) % size]) for i in rang...  3.01 us
    pallas_call x1, Pallas kernels, on_device(): pl.pallas_call(functools.partial(transport_kernel, tracers, blocks, regio...  1.99 us
    ppermute x1, waiting for transfers between devices, swapped(): return lax.ppermute(block, axis, [(i, i ^ k) for i in range(size)])  1.51 us
    pallas_call x1, Pallas kernels, on_device(): pl.pallas_call(functools.partial(pack_kernel, tracers), out_shape=(pltpu....  0.87 us
  transfers between devices with their start and end apart: 4, of which 3 were waited for; matrix products, arithmetic and copies ran while one was open for 0% of the time, Pallas kernels for 0%

profile of v6, /device:TPU:0, one launch (start us, length us, event | category | flops | bytes accessed | tf_op | source)
XLA Modules:
  0.0 14.7 jit_solution(5374058094315048431)
XLA Ops:
  0.0 0.9 %shard_map.91 = (f32[120,128]{1,0:T(8,128)S(1)}, f32[16,128]{1,0:T(8,128)S(1)}) custom-call(s32[6,2,8,128]{3,2,1,0:T(8,128)} %sign_ref.1, s32[2,128]{1,0:T(2,128)} %shift_ref.1, f32[2,128]{1,0:T(2,128)} %frac_ref.1, f32[2,128]{1,0:T(2,128)} %face_ref.1, f32[8,128]{1,0:T(8,128)} %convect_ref.1, f32[8,128]{1,0:T(8,128)} %foot_ref.1, s32[8,128]{1,0:T(8,128)} %region_ref.1), custom_call_target="tpu_custom_call" | custom-call | tf_op jit(solution)/shard_map/pallas_call | solution.py:264
  0.9 3.1 %collective-permute-start = (f32[120,128]{1,0:T(8,128)S(1)}, f32[120,128]{1,0:T(8,128)S(1)}, u32[]{:S(2)}, u32[]{:S(2)}) collective-permute-start(f32[120,128]{1,0:T(8,128)S(1)} %get-tuple-element.7), channel_id=1, source_target_pairs={{0,4},{4,12},{8,0},{12,8},{1,5},{5,13},{9,1},{13,9},{2,6},{6,14},{... | collective-permute-start | bytes 184328 | tf_op jit(solution)/shard_map/ppermute | solution.py:25
  4.0 2.5 %collective-permute-start.1 = (f32[120,128]{1,0:T(8,128)S(1)}, f32[120,128]{1,0:T(8,128)S(1)}, u32[]{:S(2)}, u32[]{:S(2)}) collective-permute-start(f32[120,128]{1,0:T(8,128)S(1)} %get-tuple-element.7), channel_id=1, source_target_pairs={{0,12},{4,8},{8,4},{12,0},{1,13},{5,9},{9,5},{13,1},{2,14},{6,10},... | collective-permute-start | bytes 184328 | tf_op jit(solution)/shard_map/ppermute | solution.py:25
  6.4 1.6 %collective-permute-start.2 = (f32[120,128]{1,0:T(8,128)S(1)}, f32[120,128]{1,0:T(8,128)S(1)}, u32[]{:S(2)}, u32[]{:S(2)}) collective-permute-start(f32[120,128]{1,0:T(8,128)S(1)} %get-tuple-element.7), channel_id=1, source_target_pairs={{0,8},{4,0},{8,12},{12,4},{1,9},{5,1},{9,13},{13,5},{2,10},{6,2},{... | collective-permute-start | bytes 184328 | tf_op jit(solution)/shard_map/ppermute | solution.py:25
  8.0 0.0 collective-permute-done
  8.0 2.7 %collective-permute-done.1 = f32[120,128]{1,0:T(8,128)S(1)} collective-permute-done((f32[120,128]{1,0:T(8,128)S(1)}, f32[120,128]{1,0:T(8,128)S(1)}, u32[]{:S(2)}, u32[]{:S(2)}) %collective-permute-start.1) | collective-permute-done | bytes 61472 | tf_op jit(solution)/shard_map/ppermute | solution.py:25
  10.7 0.3 %collective-permute-done.2 = f32[120,128]{1,0:T(8,128)S(1)} collective-permute-done((f32[120,128]{1,0:T(8,128)S(1)}, f32[120,128]{1,0:T(8,128)S(1)}, u32[]{:S(2)}, u32[]{:S(2)}) %collective-permute-start.2) | collective-permute-done | bytes 61472 | tf_op jit(solution)/shard_map/ppermute | solution.py:25
  11.1 0.0 copy-start
  11.1 0.0 copy-start.1
  11.1 0.1 collective-permute-start.3
  11.2 1.5 %collective-permute-done.3.other_ref = f32[496,128]{1,0:T(8,128)S(1)} collective-permute-done((f32[496,128]{1,0:T(8,128)S(1)}, f32[496,128]{1,0:T(8,128)S(1)}, u32[]{:S(2)}, u32[]{:S(2)}) %collective-permute-start.3) | collective-permute-done | bytes 253984 | tf_op jit(solution)/shard_map/ppermute | solution.py:15
  12.7 0.0 copy-done
  12.7 0.0 copy-done.1
  12.7 2.0 %shard_map.92 = f32[6,2,8,128]{3,2,1,0:T(8,128)} custom-call(f32[496,128]{1,0:T(8,128)S(1)} %constant_dynamic-update-slice_fusion.own_ref, f32[496,128]{1,0:T(8,128)S(1)} %collective-permute-done.3.other_ref, s32[1,32]{1,0:T(1,128)S(1)} %bitcast.1, f32[6,32]{1,0:T(8,128)S(1)} %copy-done), custom_call_target="tpu_custom_call" | custom-call | tf_op jit(solution)/shard_map/pallas_call | solution.py:273
  (5 shorter events, 0.0 us)
Async XLA Ops:
  0.9 7.1 %collective-permute-start = (f32[120,128]{1,0:T(8,128)S(1)}, f32[120,128]{1,0:T(8,128)S(1)}, u32[]{:S(2)}, u32[]{:S(2)}) collective-permute-start(f32[120,128]{1,0:T(8,128)S(1)} %get-tuple-element.7), channel_id=1, source_target_pairs={{0,4},{4,12},{8,0},{12,8},{1,5},{5,13},{9,1},{13,9},{2,6},{6,14},{... | collective-permute-start | bytes 184328 | tf_op jit(solution)/shard_map/ppermute | solution.py:25
  4.0 6.8 %collective-permute-start.1 = (f32[120,128]{1,0:T(8,128)S(1)}, f32[120,128]{1,0:T(8,128)S(1)}, u32[]{:S(2)}, u32[]{:S(2)}) collective-permute-start(f32[120,128]{1,0:T(8,128)S(1)} %get-tuple-element.7), channel_id=1, source_target_pairs={{0,12},{4,8},{8,4},{12,0},{1,13},{5,9},{9,5},{13,1},{2,14},{6,10},... | collective-permute-start | bytes 184328 | tf_op jit(solution)/shard_map/ppermute | solution.py:25
  6.4 4.6 %collective-permute-start.2 = (f32[120,128]{1,0:T(8,128)S(1)}, f32[120,128]{1,0:T(8,128)S(1)}, u32[]{:S(2)}, u32[]{:S(2)}) collective-permute-start(f32[120,128]{1,0:T(8,128)S(1)} %get-tuple-element.7), channel_id=1, source_target_pairs={{0,8},{4,0},{8,12},{12,4},{1,9},{5,1},{9,13},{13,5},{2,10},{6,2},{... | collective-permute-start | bytes 184328 | tf_op jit(solution)/shard_map/ppermute | solution.py:25
  11.1 1.6 %copy-start = (f32[6,32]{1,0:T(8,128)S(1)}, f32[6,32]{1,0:T(8,128)}, u32[]{:S(2)}) copy-start(f32[6,32]{1,0:T(8,128)} %prior_ref.1) | copy-start | bytes 2308
  11.1 1.6 %copy-start.1 = (s32[32]{0:T(128)S(1)}, s32[32]{0:T(128)}, u32[]{:S(2)}) copy-start(s32[32]{0:T(128)} %param.16) | copy-start | bytes 388
  11.1 1.6 %collective-permute-start.3 = (f32[496,128]{1,0:T(8,128)S(1)}, f32[496,128]{1,0:T(8,128)S(1)}, u32[]{:S(2)}, u32[]{:S(2)}) collective-permute-start(f32[496,128]{1,0:T(8,128)S(1)} %constant_dynamic-update-slice_fusion.own_ref), channel_id=1, source_target_pairs={{0,2},{2,0},{1,3},{3,1},{4,6},{6,4},{5,7},{7,5},{8,10},{10,8},{9,1... | collective-permute-start | bytes 761864 | tf_op jit(solution)/shard_map/ppermute | solution.py:15

commit v7 on v6

--- a/solution.py
+++ b/solution.py
@@ -54,12 +54,10 @@
     )
 
     def north(v):
-        r = [pltpu.roll(x, LANES - 1, 1) for x in v]
-        return [jnp.where(last_lane, r[1], r[0]), jnp.where(last_lane, r[0], r[1])]
+        return [pltpu.roll(jnp.where(first_lane, v[1 - h], v[h]), LANES - 1, 1) for h in range(2)]
 
     def south(v):
-        r = [pltpu.roll(x, 1, 1) for x in v]
-        return [jnp.where(first_lane, r[1], r[0]), jnp.where(first_lane, r[0], r[1])]
+        return [pltpu.roll(jnp.where(last_lane, v[1 - h], v[h]), 1, 1) for h in range(2)]
 
     face_prev = [south(x) for x in face]
     face_mid = [[1.0 - face[l][h] - face_prev[l][h] for h in range(2)] for l in range(2)]

time: 14.8 us -> 14.8 us (level)
  no operation moved by 1% of the time
where the time goes in v7:
time: 14.8 us; the launch traced here: 14.7 us
  starting transfers between devices  7.2 us (49%)
  waiting for transfers between devices  4.52 us (31%)
  Pallas kernels  2.86 us (19%)
    ppermute x3, starting transfers between devices, turned(): lax.ppermute(block, 'lon', [(i, spot[(ring(i) + k) % size]) for i in rang...  7.13 us
    ppermute x3, waiting for transfers between devices, turned(): lax.ppermute(block, 'lon', [(i, spot[(ring(i) + k) % size]) for i in rang...  3.01 us
    pallas_call x1, Pallas kernels, on_device(): pl.pallas_call(functools.partial(transport_kernel, tracers, blocks, regio...  2 us
    ppermute x1, waiting for transfers between devices, swapped(): return lax.ppermute(block, axis, [(i, i ^ k) for i in range(size)])  1.51 us
    pallas_call x1, Pallas kernels, on_device(): pl.pallas_call(functools.partial(pack_kernel, tracers), out_shape=(pltpu....  0.87 us
  transfers between devices with their start and end apart: 4, of which 3 were waited for; matrix products, arithmetic and copies ran while one was open for 0% of the time, Pallas kernels for 0%

profile of v7, /device:TPU:0, one launch (start us, length us, event | category | flops | bytes accessed | tf_op | source)
XLA Modules:
  0.0 14.7 jit_solution(8371214119414570067)
XLA Ops:
  0.0 0.9 %shard_map.91 = (f32[120,128]{1,0:T(8,128)S(1)}, f32[16,128]{1,0:T(8,128)S(1)}) custom-call(s32[6,2,8,128]{3,2,1,0:T(8,128)} %sign_ref.1, s32[2,128]{1,0:T(2,128)} %shift_ref.1, f32[2,128]{1,0:T(2,128)} %frac_ref.1, f32[2,128]{1,0:T(2,128)} %face_ref.1, f32[8,128]{1,0:T(8,128)} %convect_ref.1, f32[8,128]{1,0:T(8,128)} %foot_ref.1, s32[8,128]{1,0:T(8,128)} %region_ref.1), custom_call_target="tpu_custom_call" | custom-call | tf_op jit(solution)/shard_map/pallas_call | solution.py:262
  0.9 3.1 %collective-permute-start = (f32[120,128]{1,0:T(8,128)S(1)}, f32[120,128]{1,0:T(8,128)S(1)}, u32[]{:S(2)}, u32[]{:S(2)}) collective-permute-start(f32[120,128]{1,0:T(8,128)S(1)} %get-tuple-element.7), channel_id=1, source_target_pairs={{0,4},{4,12},{8,0},{12,8},{1,5},{5,13},{9,1},{13,9},{2,6},{6,14},{... | collective-permute-start | bytes 184328 | tf_op jit(solution)/shard_map/ppermute | solution.py:25
  4.0 2.5 %collective-permute-start.1 = (f32[120,128]{1,0:T(8,128)S(1)}, f32[120,128]{1,0:T(8,128)S(1)}, u32[]{:S(2)}, u32[]{:S(2)}) collective-permute-start(f32[120,128]{1,0:T(8,128)S(1)} %get-tuple-element.7), channel_id=1, source_target_pairs={{0,12},{4,8},{8,4},{12,0},{1,13},{5,9},{9,5},{13,1},{2,14},{6,10},... | collective-permute-start | bytes 184328 | tf_op jit(solution)/shard_map/ppermute | solution.py:25
  6.4 1.6 %collective-permute-start.2 = (f32[120,128]{1,0:T(8,128)S(1)}, f32[120,128]{1,0:T(8,128)S(1)}, u32[]{:S(2)}, u32[]{:S(2)}) collective-permute-start(f32[120,128]{1,0:T(8,128)S(1)} %get-tuple-element.7), channel_id=1, source_target_pairs={{0,8},{4,0},{8,12},{12,4},{1,9},{5,1},{9,13},{13,5},{2,10},{6,2},{... | collective-permute-start | bytes 184328 | tf_op jit(solution)/shard_map/ppermute | solution.py:25
  8.0 0.0 collective-permute-done
  8.0 2.7 %collective-permute-done.1 = f32[120,128]{1,0:T(8,128)S(1)} collective-permute-done((f32[120,128]{1,0:T(8,128)S(1)}, f32[120,128]{1,0:T(8,128)S(1)}, u32[]{:S(2)}, u32[]{:S(2)}) %collective-permute-start.1) | collective-permute-done | bytes 61472 | tf_op jit(solution)/shard_map/ppermute | solution.py:25
  10.7 0.3 %collective-permute-done.2 = f32[120,128]{1,0:T(8,128)S(1)} collective-permute-done((f32[120,128]{1,0:T(8,128)S(1)}, f32[120,128]{1,0:T(8,128)S(1)}, u32[]{:S(2)}, u32[]{:S(2)}) %collective-permute-start.2) | collective-permute-done | bytes 61472 | tf_op jit(solution)/shard_map/ppermute | solution.py:25
  11.1 0.0 copy-start
  11.1 0.0 copy-start.1
  11.1 0.1 collective-permute-start.3
  11.2 1.5 %collective-permute-done.3.other_ref = f32[496,128]{1,0:T(8,128)S(1)} collective-permute-done((f32[496,128]{1,0:T(8,128)S(1)}, f32[496,128]{1,0:T(8,128)S(1)}, u32[]{:S(2)}, u32[]{:S(2)}) %collective-permute-start.3) | collective-permute-done | bytes 253984 | tf_op jit(solution)/shard_map/ppermute | solution.py:15
  12.7 0.0 copy-done
  12.7 0.0 copy-done.1
  12.7 2.0 %shard_map.92 = f32[6,2,8,128]{3,2,1,0:T(8,128)} custom-call(f32[496,128]{1,0:T(8,128)S(1)} %constant_dynamic-update-slice_fusion.own_ref, f32[496,128]{1,0:T(8,128)S(1)} %collective-permute-done.3.other_ref, s32[1,32]{1,0:T(1,128)S(1)} %bitcast.1, f32[6,32]{1,0:T(8,128)S(1)} %copy-done), custom_call_target="tpu_custom_call" | custom-call | tf_op jit(solution)/shard_map/pallas_call | solution.py:271
  (5 shorter events, 0.0 us)
Async XLA Ops:
  0.9 7.1 %collective-permute-start = (f32[120,128]{1,0:T(8,128)S(1)}, f32[120,128]{1,0:T(8,128)S(1)}, u32[]{:S(2)}, u32[]{:S(2)}) collective-permute-start(f32[120,128]{1,0:T(8,128)S(1)} %get-tuple-element.7), channel_id=1, source_target_pairs={{0,4},{4,12},{8,0},{12,8},{1,5},{5,13},{9,1},{13,9},{2,6},{6,14},{... | collective-permute-start | bytes 184328 | tf_op jit(solution)/shard_map/ppermute | solution.py:25
  4.0 6.8 %collective-permute-start.1 = (f32[120,128]{1,0:T(8,128)S(1)}, f32[120,128]{1,0:T(8,128)S(1)}, u32[]{:S(2)}, u32[]{:S(2)}) collective-permute-start(f32[120,128]{1,0:T(8,128)S(1)} %get-tuple-element.7), channel_id=1, source_target_pairs={{0,12},{4,8},{8,4},{12,0},{1,13},{5,9},{9,5},{13,1},{2,14},{6,10},... | collective-permute-start | bytes 184328 | tf_op jit(solution)/shard_map/ppermute | solution.py:25
  6.4 4.6 %collective-permute-start.2 = (f32[120,128]{1,0:T(8,128)S(1)}, f32[120,128]{1,0:T(8,128)S(1)}, u32[]{:S(2)}, u32[]{:S(2)}) collective-permute-start(f32[120,128]{1,0:T(8,128)S(1)} %get-tuple-element.7), channel_id=1, source_target_pairs={{0,8},{4,0},{8,12},{12,4},{1,9},{5,1},{9,13},{13,5},{2,10},{6,2},{... | collective-permute-start | bytes 184328 | tf_op jit(solution)/shard_map/ppermute | solution.py:25
  11.1 1.6 %copy-start = (f32[6,32]{1,0:T(8,128)S(1)}, f32[6,32]{1,0:T(8,128)}, u32[]{:S(2)}) copy-start(f32[6,32]{1,0:T(8,128)} %prior_ref.1) | copy-start | bytes 2308
  11.1 1.6 %copy-start.1 = (s32[32]{0:T(128)S(1)}, s32[32]{0:T(128)}, u32[]{:S(2)}) copy-start(s32[32]{0:T(128)} %param.16) | copy-start | bytes 388
  11.1 1.6 %collective-permute-start.3 = (f32[496,128]{1,0:T(8,128)S(1)}, f32[496,128]{1,0:T(8,128)S(1)}, u32[]{:S(2)}, u32[]{:S(2)}) collective-permute-start(f32[496,128]{1,0:T(8,128)S(1)} %constant_dynamic-update-slice_fusion.own_ref), channel_id=1, source_target_pairs={{0,2},{2,0},{1,3},{3,1},{4,6},{6,4},{5,7},{7,5},{8,10},{10,8},{9,1... | collective-permute-start | bytes 761864 | tf_op jit(solution)/shard_map/ppermute | solution.py:15
